TPU v7x, 128 devices: a whole 4x4x4 slice. The times are simulated.
128 devices in a mesh: dp: 4 (over y), ctx: 32 (over z, x, core).
Axes of the slice: x: 4, y: 4, z: 4, core: 2. Of those that a mesh axis runs over, the one named last changes fastest.
Arguments:
- tokens: bfloat16 [4, 20480, 4096], P('dp', 'ctx'), may hold values from -400 to 400
- w_query: bfloat16 [4096, 1024], P(('dp', 'ctx')), may hold values from -0.09375 to 0.09375
- w_key: bfloat16 [4096, 1024], P(('dp', 'ctx')), may hold values from -0.09375 to 0.09375
- w_value: bfloat16 [4096, 2048], P(('dp', 'ctx')), may hold values from -0.09375 to 0.09375
- w_gates: bfloat16 [4096, 8], P(('dp', 'ctx')), may hold values from -0.09375 to 0.09375
- forget_bias: float32 [4], replicated, may hold values from 2 to 15
- doc_lengths: int32 [4, 16], P('dp'), may hold values from 1 to 10240, 20480 in all within a row
Outputs:
- head_out: bfloat16 [4, 20480, 2048], P('dp', 'ctx')
Inputs may be any that keep to these rules, and one draw needn't show every extreme that they name: `doc_lengths`: each sequence's 16 lengths sum to 20480; the longest is exactly 10240.
All inputs are finite; a program needn't handle non-finite values.
Results may differ from a plain program's by a relative error of at most 0.025.
Values may be sent and summed in bfloat16 or wider, within the bound.
No kernel may reach another device: no remote copies, remote signals or barrier semaphores. Data moves between devices by JAX's collectives and lax.ppermute only.
A program may use at most 128 MiB of HBM per device.

v0:
```python
import jax
import jax.numpy as jnp
from jax import lax
from jax.sharding import PartitionSpec as P


def entering(value, axis, join, neutral):
    count, mine = (lax.axis_size(axis), lax.axis_index(axis))
    pieces = jax.tree.map(lambda part: lax.all_gather(part, axis), value)
    running = jax.tree.map(
        lambda part, zero: jnp.full_like(part, 0) + jnp.asarray(zero, part.dtype), value, neutral
    )

    def turn(position, running):
        longer = join(running, jax.tree.map(lambda part: part[position], pieces))
        return jax.tree.map(lambda new, old: jnp.where(position < mine, new, old), longer, running)

    return lax.fori_loop(0, count - 1, turn, running)


def normalize(block):
    values = block.astype(jnp.float32)
    scale = lax.rsqrt(jnp.mean(values * values, axis=-1, keepdims=True) + 1e-06)
    return (values * scale).astype(jnp.bfloat16)


def gate_terms(gates, forget_bias, resets):
    heads = forget_bias.shape[0]
    in_gate = gates[:, :heads]
    log_forget = jax.nn.log_sigmoid(gates[:, heads:] + forget_bias[None, :])
    cumul = jnp.cumsum(log_forget, axis=0)
    segment = jnp.cumsum(resets.astype(jnp.int32))
    return (in_gate, cumul, segment)


def shard_state(keys, values, in_gate, cumul, segment):
    rows = keys.shape[0]
    heads = in_gate.shape[1]
    keys3 = keys.reshape(rows, heads, -1)
    value_rows3 = values.reshape(rows, heads, -1)
    last = cumul[-1]
    same = (segment == segment[-1])[:, None]
    weight = jnp.exp(jnp.where(same, last[None, :] - cumul + in_gate, -1e30))
    scaled_values = (keys3 * weight[:, :, None]).astype(jnp.bfloat16)
    memory_state = jnp.einsum(
        "bdy,bdr->dyr", scaled_values, value_rows3, preferred_element_type=jnp.float32
    )
    decay = jnp.exp(last) * (segment[-1] == 0).astype(jnp.float32)
    return (decay.astype(jnp.bfloat16), memory_state.astype(jnp.bfloat16))


def shard_output(queries, keys, values, in_gate, cumul, segment, carried_state):
    rows = queries.shape[0]
    heads = in_gate.shape[1]
    query_rows3 = queries.reshape(rows, heads, -1)
    keys3 = keys.reshape(rows, heads, -1)
    value_rows3 = values.reshape(rows, heads, -1)
    decay_factor = 1.0 / jnp.sqrt(jnp.float32(query_rows3.shape[2]))
    scores = (
        jnp.einsum("thk,shk->hts", query_rows3, keys3, preferred_element_type=jnp.float32)
        * decay_factor
    )
    order = jnp.arange(rows, dtype=jnp.int32)
    mask = (order[:, None] >= order[None, :]) & (segment[:, None] == segment[None, :])
    diff = cumul.T[:, :, None] - cumul.T[:, None, :] + in_gate.T[:, None, :]
    mixed = (scores * jnp.exp(jnp.where(mask[None], diff, -1e30))).astype(jnp.bfloat16)
    intra = jnp.einsum("hts,shv->thv", mixed, value_rows3, preferred_element_type=jnp.float32)
    decay_reach = jnp.exp(cumul) * (segment == 0).astype(jnp.float32)[:, None]
    between_shards = (
        jnp.einsum("wia,iax->wix", query_rows3, carried_state, preferred_element_type=jnp.float32)
        * (decay_reach * decay_factor)[:, :, None]
    )
    readout = intra + between_shards
    scale = lax.rsqrt(jnp.mean(readout * readout, axis=-1, keepdims=True) + 1e-05)
    return (readout * scale).astype(jnp.bfloat16).reshape(rows, -1)


def combine(earlier, later):
    decay_early, state_early = earlier
    decay_late, state_late = later
    decay_f = decay_late.astype(jnp.float32)
    joined = (decay_early.astype(jnp.float32) * decay_f).astype(jnp.bfloat16)
    merged = decay_f[:, None, None] * state_early.astype(jnp.float32) + state_late.astype(
        jnp.float32
    )
    return (joined, merged.astype(jnp.bfloat16))


def carry_in(decay, memory_state):
    identity = (jnp.ones_like(decay), jnp.zeros_like(memory_state))
    prior = entering((decay, memory_state), "ctx", combine, identity)
    return prior[1]


def per_device(tokens, w_query, w_key, w_value, w_gates, forget_bias, doc_lengths):
    normed = normalize(tokens[0])
    rows = normed.shape[0]
    lengths = doc_lengths[0]
    starts = jnp.cumsum(lengths) - lengths
    positions = lax.axis_index("ctx") * rows + jnp.arange(rows, dtype=jnp.int32)
    resets = jnp.any(positions[:, None] == starts[None, :], axis=1)
    pieces = (
        lax.all_gather(w_query, ("dp", "ctx"), axis=0, tiled=True),
        lax.all_gather(w_key, ("dp", "ctx"), axis=0, tiled=True),
        lax.all_gather(w_value, ("dp", "ctx"), axis=0, tiled=True),
        lax.all_gather(w_gates, ("dp", "ctx"), axis=0, tiled=True),
    )
    query_acc, key_acc, value_acc, gates = tuple(
        (jnp.dot(normed, piece, preferred_element_type=jnp.float32) for piece in pieces)
    )
    queries = query_acc.astype(jnp.bfloat16)
    keys = key_acc.astype(jnp.bfloat16)
    values = value_acc.astype(jnp.bfloat16)
    in_gate, cumul, segment = gate_terms(gates, forget_bias, resets)
    decay, memory_state = shard_state(keys, values, in_gate, cumul, segment)
    carried_state = carry_in(decay, memory_state)
    result = shard_output(queries, keys, values, in_gate, cumul, segment, carried_state)
    return result.reshape(1, rows, -1)


def solution(mesh):
    in_specs = (
        P("dp", "ctx", None),
        P(("dp", "ctx"), None),
        P(("dp", "ctx"), None),
        P(("dp", "ctx"), None),
        P(("dp", "ctx"), None),
        P(),
        P("dp", None),
    )
    out_specs = P("dp", "ctx", None)
    return jax.shard_map(
        per_device, mesh=mesh, in_specs=in_specs, out_specs=out_specs, check_vma=False
    )
```

profile of v0, /device:TPU:25, one launch (start us, length us, event | category | flops | bytes accessed | tf_op | source)
XLA Modules:
  0.0 424.2 jit_solution(17067810681525082466)
XLA Ops:
  10.8 37.3 %all-gather.1 = bf16[128,32,8]{1,2,0:T(8,128)(2,1)S(1)} all-gather(bf16[1,32,8]{1,2,0:T(8,128)(2,1)} %bitcast.86), channel_id=1, replica_groups=mesh['dp'=4,'ctx'=32] {'dp','ctx'}, dimensions={0}, use_global_device_ids=true | all-gather | bytes 66048 | tf_op jit(solution)/shard_map/all_gather | solution.py:106
  48.4 3.7 fusion.2
  52.5 1.5 fusion.36
  57.4 24.1 %all-gather.12.cloned.1.call-done = bf16[4096,1024]{1,0:T(8,128)(2,1)} async-done(((bf16[32,1024]{1,0:T(8,128)(2,1)}), bf16[4096,1024]{1,0:T(8,128)(2,1)}) %all-gather.12.cloned.1.call-update) | async-done | bytes 8388624 | tf_op jit(solution)/shard_map/all_gather | solution.py:104
  81.5 10.1 %convolution_convert_fusion.1 = bf16[640,1024]{1,0:T(8,128)(2,1)S(1)} fusion(bf16[4096,1024]{1,0:T(8,128)(2,1)} %all-gather.12.cloned.1.call-done, bf16[1,640,4096]{2,1,0:T(8,128)(2,1)} %param.9, f32[640]{0:T(1024)S(1)} %add_rsqrt_fusion.1), kind=kOutput, calls=%fused_computation.30 | convolution fusion | flops 5377228800 | bytes 14944768 | tf_op jit(solution)/shard_map/dot_general | solution.py:109
  92.4 71.7 %all-gather.8.cloned.1.call-done = bf16[4096,2048]{1,0:T(8,128)(2,1)} async-done(((bf16[32,2048]{1,0:T(8,128)(2,1)}), bf16[4096,2048]{1,0:T(8,128)(2,1)}) %all-gather.8.cloned.1.call-update) | async-done | bytes 16777232 | tf_op jit(solution)/shard_map/all_gather | solution.py:105
  164.1 16.1 %convolution_convert_fusion = bf16[640,2048]{1,0:T(8,128)(2,1)S(1)} fusion(bf16[4096,2048]{1,0:T(8,128)(2,1)} %all-gather.8.cloned.1.call-done, bf16[1,640,4096]{2,1,0:T(8,128)(2,1)} %param.9, f32[640]{0:T(1024)S(1)} %add_rsqrt_fusion.1), kind=kOutput, calls=%fused_computation.20 | convolution fusion | flops 10746593280 | bytes 24644096 | tf_op jit(solution)/shard_map/dot_general | solution.py:109
  180.3 1.5 copy-done.3
  181.8 2.1 fusion.20
  184.6 21.1 %all-gather.2 = bf16[32,1,4]{2,1,0:T(2,128)(2,1)S(1)} all-gather(bf16[1,1,4]{2,1,0:T(2,128)(2,1)S(1)} %bitcast.87), channel_id=1, replica_groups=mesh['dp'=4,'ctx'=32] {'ctx'}, dimensions={0}, use_global_device_ids=true | all-gather | bytes 264 | tf_op jit(solution)/shard_map/all_gather | solution.py:9
  206.2 29.0 %all-gather.10.cloned.1.call-done = bf16[4096,1024]{1,0:T(8,128)(2,1)} async-done(((bf16[32,1024]{1,0:T(8,128)(2,1)}), bf16[4096,1024]{1,0:T(8,128)(2,1)}) %all-gather.10.cloned.1.call-update) | async-done | bytes 8388624 | tf_op jit(solution)/shard_map/all_gather | solution.py:103
  235.2 10.1 %convolution_convert_fusion.2 = bf16[640,1024]{1,0:T(8,128)(2,1)S(1)} fusion(bf16[4096,1024]{1,0:T(8,128)(2,1)} %all-gather.10.cloned.1.call-done, bf16[1,640,4096]{2,1,0:T(8,128)(2,1)} %param.9, f32[640]{0:T(1024)S(1)} %add_rsqrt_fusion.1), kind=kOutput, calls=%fused_computation.31 | convolution fusion | flops 5377228800 | bytes 14944768 | tf_op jit(solution)/shard_map/dot_general | solution.py:109
  245.3 9.8 %fusion.5 = f32[4,512,640]{2,1,0:T(8,128)} fusion(f32[4,640]{1,0:T(4,128)S(1)} %get-tuple-element.153, f32[4,640]{1,0:T(4,128)S(1)} %get-tuple-element.149, pred[640,640]{1,0:T(8,128)(4,1)S(1)} %fusion.19, bf16[640,4,256]{0,2,1:T(8,128)(2,1)} %bitcast.80, bf16[80,4,8,512]{3,2,1,0:T(8,128)(2,1)} %bitcast.89, bf16[80,4,8,256]{3,2,1,0:T(8,128)(2,1)S(1)} %bitcast.77), kind=kOutput, calls=%fused_computation.13 | convolution fusion | flops 2526412800 | bytes 10915840 | tf_op jit(solution)/shard_map/hts,shv->thv/dot_general | solution.py:67
  255.1 95.3 %all-gather.14.cloned.1.call-done = bf16[128,256,512]{2,1,0:T(8,128)(2,1)} async-done(((bf16[4,256,512]{2,1,0:T(8,128)(2,1)}), bf16[128,256,512]{2,1,0:T(8,128)(2,1)}) %all-gather.14.cloned.1.call-update) | async-done | bytes 33554448 | tf_op jit(solution)/shard_map/all_gather | solution.py:9
  350.4 60.2 %while.14 = (s32[]{:T(128)}, bf16[4,256,512]{2,1,0:T(8,128)(2,1)S(1)}, s32[]{:T(128)}, bf16[32,4]{1,0:T(8,128)(2,1)S(1)}, bf16[32,4,256,512]{3,2,1,0:T(8,128)(2,1)}, /*index=5*/s32[]{:T(128)}, s32[]{:T(128)}) while((s32[]{:T(128)}, bf16[4,256,512]{2,1,0:T(8,128)(2,1)S(1)}, s32[]{:T(128)}, bf16[32,4]{1,0:T(8,128)(2,1)S(1)}, ...), condition=%wide.region_8.9_spmd.clone, body=%wide.region_7.8_spmd.clone.sunk | while | flops 3670024 | bytes 3145881 | solution.py:18
  350.4 1.9 fusion.48
  352.4 1.9 fusion.48
  354.3 1.9 fusion.48
  356.2 1.9 fusion.48
  358.2 1.9 fusion.48
  360.1 1.9 fusion.48
  362.1 1.9 fusion.48
  364.0 1.9 fusion.48
  366.0 1.9 fusion.48
  367.9 1.9 fusion.48
  369.8 1.9 fusion.48
  371.8 1.9 fusion.48
  373.7 1.9 fusion.48
  375.7 1.9 fusion.48
  377.6 1.9 fusion.48
  379.6 1.9 fusion.48
  381.5 1.9 fusion.48
  383.4 1.9 fusion.48
  385.4 1.9 fusion.48
  387.3 1.9 fusion.48
  389.3 1.9 fusion.48
  391.2 1.9 fusion.48
  393.1 1.9 fusion.48
  395.1 1.9 fusion.48
  397.0 1.9 fusion.48
  399.0 1.9 fusion.48
  400.9 1.9 fusion.48
  402.9 1.9 fusion.48
  404.8 1.9 fusion.48
  406.7 1.9 fusion.48
  408.7 1.9 fusion.48
  410.6 3.9 multiply_reduce_fusion
  415.0 2.6 copy.46
  (78 shorter events, 10.4 us)
Async XLA Ops:
  6.5 75.0 %all-gather.12.cloned.1.call-start = ((), (), s32[]{:S(2)}) async-start(), calls=%async_computation.2 | async-start | bytes 8454144 | tf_op jit(solution)/shard_map/all_gather | solution.py:104
  7.3 156.9 %all-gather.8.cloned.1.call-start = ((), (), s32[]{:S(2)}) async-start(), calls=%async_computation | async-start | bytes 16908288 | tf_op jit(solution)/shard_map/all_gather | solution.py:105
  8.0 227.2 %all-gather.10.cloned.1.call-start = ((), (), s32[]{:S(2)}) async-start(), calls=%async_computation.1 | async-start | bytes 8454144 | tf_op jit(solution)/shard_map/all_gather | solution.py:103
  8.7 341.7 %all-gather.14.cloned.1.call-start = ((), (), s32[]{:S(2)}) async-start(), calls=%async_computation.3 | async-start | bytes 34603008 | tf_op jit(solution)/shard_map/all_gather | solution.py:9
  48.4 4.1 copy-start
  48.4 5.6 %copy-start.2 = (f32[4]{0:T(128)S(1)}, f32[4]{0:T(128)}, u32[]{:S(2)}) copy-start(f32[4]{0:T(128)} %param.14) | copy-start | bytes 52
  92.4 87.9 %copy-start.1 = (bf16[640,1024]{0,1:T(8,128)(2,1)}, bf16[640,1024]{0,1:T(8,128)(2,1)S(1)}, u32[]{:S(2)}) copy-start(bf16[640,1024]{0,1:T(8,128)(2,1)S(1)} %copy.48) | copy-start | bytes 3932164
  180.3 1.5 copy-start.3
Sparse Core Ops, SparseCore 0:
  10.3 71.1 all-gather.11
  84.7 79.4 all-gather.7
  167.1 68.0 all-gather.9
  237.3 113.0 all-gather.13
where the time goes:
time: 427 us; the launch traced here: 424 us
  waiting for transfers between devices  222 us (52%)
  other arithmetic  68.1 us (16%)
  blocking collectives  58.4 us (14%)
  matrix products  53.7 us (13%)
  between operations  13.9 us (3%)
  local copies, waits for them, and re-layouts  6.82 us (2%)
    all_gather x1, waiting for transfers between devices, entering(): pieces = jax.tree.map(lambda part: lax.all_gather(part, axis), value)  95.3 us
    all_gather x1, waiting for transfers between devices, per_device(): lax.all_gather(w_value, ('dp', 'ctx'), axis=0, tiled=True)  71.7 us
    select_n x31, other arithmetic, turn(): jnp.where(position < mine, new, old)  58.9 us
    dot_general x4, matrix products, per_device(): jnp.dot(normed, piece, preferred_element_type=jnp.float32)  37.9 us
    all_gather x1, blocking collectives, per_device(): lax.all_gather(w_gates, ('dp', 'ctx'), axis=0, tiled=True)  37.3 us
    all_gather x1, waiting for transfers between devices, per_device(): lax.all_gather(w_query, ('dp', 'ctx'), axis=0, tiled=True)  29 us
    all_gather x1, waiting for transfers between devices, per_device(): lax.all_gather(w_key, ('dp', 'ctx'), axis=0, tiled=True)  24.1 us
    all_gather x1, blocking collectives, entering(): pieces = jax.tree.map(lambda part: lax.all_gather(part, axis), value)  21.1 us
  transfers between devices with their start and end apart: 4, of which 4 were waited for; matrix products, arithmetic and copies ran while one was open for 14% of the time, Pallas kernels for 0%

commit v1 on v0

v1 whole, which is shorter than its diff:
```python
import functools

import jax
import jax.numpy as jnp
from jax import lax
from jax.experimental import pallas as pl
from jax.experimental.pallas import tpu as pltpu
from jax.sharding import Mesh, PartitionSpec as P

ROWS = 640
DQK = 256
DV = 512
BF = jnp.bfloat16
F32 = jnp.float32
VMEM_LIMIT = 48 * 1024 * 1024


def swap(value):
    return lax.ppermute(value, "core", [(0, 1), (1, 0)])


def shift(value, axis, by):
    return lax.ppermute(value, axis, [(i, (i + by) % 4) for i in range(4)])


def normalize(block):
    values = block.astype(F32)
    scale = lax.rsqrt(jnp.mean(values * values, axis=-1, keepdims=True) + 1e-06)
    return (values * scale).astype(BF)


def state_kernel(cols_ref, key_ref, value_ref, out_ref):
    head = pl.program_id(1)
    weight = jnp.where(head == 0, cols_ref[0, :, 4:5], cols_ref[0, :, 5:6])
    scaled = (key_ref[...].astype(F32) * weight).astype(BF)
    out_ref[0, 0] = lax.dot_general(
        scaled, value_ref[...], (((0,), (0,)), ((), ())), preferred_element_type=F32
    ).astype(BF)


def states(cols, qkv):
    return pl.pallas_call(
        state_kernel,
        grid=(2, 2),
        in_specs=[
            pl.BlockSpec((1, ROWS, 8), lambda s, h: (s, 0, 0)),
            pl.BlockSpec((ROWS, DQK), lambda s, h: (s, 2 + h)),
            pl.BlockSpec((ROWS, DV), lambda s, h: (s, 2 + h)),
        ],
        out_specs=pl.BlockSpec((1, 1, DQK, DV), lambda s, h: (s, h, 0, 0)),
        out_shape=jax.ShapeDtypeStruct((2, 2, DQK, DV), BF),
        compiler_params=pltpu.CompilerParams(vmem_limit_bytes=VMEM_LIMIT),
        cost_estimate=pl.CostEstimate(
            flops=4 * 2 * ROWS * DQK * DV, bytes_accessed=5 << 20, transcendentals=0
        ),
        name="states",
    )(cols, qkv, qkv)


def intra_kernel(cols_ref, rows_ref, query_ref, key_ref, value_ref, out_ref):
    head = pl.program_id(1)
    cumul = jnp.where(head == 0, cols_ref[0, :, 0:1], cols_ref[0, :, 1:2])
    segment = cols_ref[0, :, 6:7]
    cumul_row = jnp.where(head == 0, rows_ref[0, 0:1, :], rows_ref[0, 1:2, :])
    gate_row = jnp.where(head == 0, rows_ref[0, 2:3, :], rows_ref[0, 3:4, :])
    segment_row = rows_ref[0, 4:5, :]
    for start, size in ((0, 256), (256, 384)):
        reach = start + size
        scores = lax.dot_general(
            query_ref[start:reach, :],
            key_ref[:reach, :],
            (((1,), (1,)), ((), ())),
            preferred_element_type=F32,
        ) * (DQK**-0.5)
        later = start + lax.broadcasted_iota(jnp.int32, (size, reach), 0)
        earlier = lax.broadcasted_iota(jnp.int32, (size, reach), 1)
        keep = (later >= earlier) & (segment[start:reach] == segment_row[:, :reach])
        diff = cumul[start:reach] - cumul_row[:, :reach] + gate_row[:, :reach]
        mixed = (scores * jnp.exp(jnp.where(keep, diff, -1e30))).astype(BF)
        out_ref[start:reach, :] = jnp.dot(
            mixed, value_ref[:reach, :], preferred_element_type=F32
        )


def intra(cols, rows, qkv):
    return pl.pallas_call(
        intra_kernel,
        grid=(2, 2),
        in_specs=[
            pl.BlockSpec((1, ROWS, 8), lambda s, h: (s, 0, 0)),
            pl.BlockSpec((1, 8, ROWS), lambda s, h: (s, 0, 0)),
            pl.BlockSpec((ROWS, DQK), lambda s, h: (s, h)),
            pl.BlockSpec((ROWS, DQK), lambda s, h: (s, 2 + h)),
            pl.BlockSpec((ROWS, DV), lambda s, h: (s, 2 + h)),
        ],
        out_specs=pl.BlockSpec((ROWS, DV), lambda s, h: (s, h)),
        out_shape=jax.ShapeDtypeStruct((2 * ROWS, 2 * DV), F32),
        compiler_params=pltpu.CompilerParams(vmem_limit_bytes=VMEM_LIMIT),
        cost_estimate=pl.CostEstimate(
            flops=4 * 2 * ROWS * ROWS * (DQK + DV),
            bytes_accessed=12 << 20,
            transcendentals=4 * ROWS * ROWS,
        ),
        name="intra",
    )(cols, rows, qkv, qkv, qkv)


def readout_kernel(cols_ref, query_ref, intra_ref, carried_ref, out_ref):
    head = pl.program_id(0)
    reach = jnp.where(head == 0, cols_ref[0, :, 2:3], cols_ref[0, :, 3:4])
    between = jnp.dot(query_ref[...], carried_ref[0], preferred_element_type=F32) * reach
    readout = intra_ref[...] + between
    scale = lax.rsqrt(jnp.mean(readout * readout, axis=-1, keepdims=True) + 1e-05)
    out_ref[...] = (readout * scale).astype(BF)


def readout(slot, cols, qkv, inner, carried):
    return pl.pallas_call(
        readout_kernel,
        grid=(2,),
        in_specs=[
            pl.BlockSpec((1, ROWS, 8), lambda h: (slot, 0, 0)),
            pl.BlockSpec((ROWS, DQK), lambda h: (slot, h)),
            pl.BlockSpec((ROWS, DV), lambda h: (slot, h)),
            pl.BlockSpec((1, DQK, DV), lambda h: (h, 0, 0)),
        ],
        out_specs=pl.BlockSpec((ROWS, DV), lambda h: (0, h)),
        out_shape=jax.ShapeDtypeStruct((ROWS, 2 * DV), BF),
        compiler_params=pltpu.CompilerParams(vmem_limit_bytes=VMEM_LIMIT),
        cost_estimate=pl.CostEstimate(
            flops=2 * 2 * ROWS * DQK * DV, bytes_accessed=5 << 20, transcendentals=0
        ),
        name="readout",
    )(cols, qkv, inner, carried)


def join(decay, earlier, later):
    return (decay.astype(F32)[:, None, None] * earlier.astype(F32) + later.astype(F32)).astype(BF)


def times(left, right):
    return (left.astype(F32) * right.astype(F32)).astype(BF)


def pack(state, decay):
    tail = jnp.broadcast_to(decay[:, None, None], (2, 8, DV))
    return jnp.concatenate([state, tail], axis=1)


def unpack(message):
    return message[:, :-8], message[:, -1, 0]


def in_order(mine, axis, send):
    place = lax.axis_index(axis)
    blocks = [mine] + [shift(send(by), axis, by) for by in (1, 2, 3)]
    stacked = jnp.stack(blocks)
    return [lax.dynamic_index_in_dim(stacked, (place - j) % 4, 0, False) for j in range(4)]


def carry_in(decay, state):
    x, z = lax.axis_index("x"), lax.axis_index("z")
    quarters = state.reshape(2, 4, DQK // 4, DV)

    def piece(by):
        return pack(lax.dynamic_index_in_dim(quarters, (x + by) % 4, 1, False), decay)

    line = [unpack(block) for block in in_order(piece(0), "x", piece)]
    prior = jnp.zeros_like(line[0][0])
    reach = jnp.ones_like(decay)
    priors, reaches = [], []
    for block, fade in line:
        priors.append(prior)
        reaches.append(reach)
        prior = join(fade, prior, block)
        reach = times(fade, reach)
    whole = pack(prior, reach)
    before = jnp.zeros_like(prior)
    for j, message in enumerate(in_order(whole, "z", lambda by: whole)):
        block, fade = unpack(message)
        before = jnp.where(j < z, join(fade, before, block), before)
    backs = jnp.stack([join(reaches[j], before, priors[j]) for j in range(4)])

    def back(by):
        return lax.dynamic_index_in_dim(backs, (x + by) % 4, 0, False)

    return jnp.stack(in_order(back(0), "x", back), axis=1).reshape(2, DQK, DV)


def per_device(tokens, w_query, w_key, w_value, w_gates, forget_bias, doc_lengths):
    core = lax.axis_index("core")
    chip = lax.axis_index("z") * 4 + lax.axis_index("x")

    def columns(which):
        def part(weight):
            width = weight.shape[1] // 2
            return lax.dynamic_slice_in_dim(weight, which * width, width, 1)

        gates = w_gates.reshape(-1, 2, 2, 2)
        gates = lax.dynamic_index_in_dim(gates, which, 2, False).reshape(-1, 4)
        gates = jnp.pad(gates, ((0, 0), (0, 124)))
        return jnp.concatenate([part(w_query), part(w_key), part(w_value), gates], axis=1)

    mine, theirs = columns(core), swap(columns(1 - core))
    block = jnp.where(
        core == 0,
        jnp.concatenate([mine, theirs], axis=0),
        jnp.concatenate([theirs, mine], axis=0),
    )
    weights = lax.all_gather(block, ("y", "z", "x"), axis=0, tiled=True)

    normed = normalize(tokens[0])
    normed = jnp.concatenate([normed, swap(normed)], axis=0)
    qkv = jnp.dot(normed, weights[:, :2048], preferred_element_type=F32).astype(BF)
    gates = jnp.dot(normed, weights[:, 2048:], preferred_element_type=F32)

    gates = gates[:, :4].reshape(2, ROWS, 4)
    lengths = doc_lengths[0]
    starts = jnp.cumsum(lengths) - lengths
    shard = chip * 2 + jnp.stack([core, 1 - core])
    positions = shard[:, None] * ROWS + jnp.arange(ROWS, dtype=jnp.int32)[None, :]
    resets = jnp.any(positions[:, :, None] == starts[None, None, :], axis=-1)
    bias = lax.dynamic_slice_in_dim(forget_bias, core * 2, 2)
    in_gate = gates[:, :, :2]
    cumul = jnp.cumsum(jax.nn.log_sigmoid(gates[:, :, 2:] + bias), axis=1)
    segment = jnp.cumsum(resets.astype(jnp.int32), axis=1)
    last = cumul[:, -1]
    same = (segment == segment[:, -1:])[:, :, None]
    weight = jnp.exp(jnp.where(same, last[:, None, :] - cumul + in_gate, -1e30))
    decay = (jnp.exp(last) * (segment[:, -1:] == 0).astype(F32)).astype(BF)
    reach = jnp.exp(cumul) * (segment == 0).astype(F32)[:, :, None] * (DQK**-0.5)
    seg = segment.astype(F32)[:, :, None]
    cols = jnp.concatenate([cumul, reach, weight, seg, jnp.zeros_like(seg)], axis=2)
    rows = jnp.concatenate([cumul, in_gate, seg, jnp.zeros_like(seg), weight], axis=2)
    rows = rows.transpose(0, 2, 1)

    state = states(cols, qkv)
    first = lax.dynamic_index_in_dim(state, core, 0, False)
    second = lax.dynamic_index_in_dim(state, 1 - core, 0, False)
    fade_first = lax.dynamic_index_in_dim(decay, core, 0, False)
    fade_second = lax.dynamic_index_in_dim(decay, 1 - core, 0, False)
    carried = carry_in(times(fade_first, fade_second), join(fade_second, first, second))
    inner = intra(cols, rows, qkv)
    carried_second = join(fade_first, carried, first)
    own = jnp.where(core == 0, carried, carried_second)
    other = jnp.where(core == 0, carried_second, carried)
    outgoing = readout(1, cols, qkv, inner, other)
    incoming = swap(outgoing)
    kept = readout(0, cols, qkv, inner, own)
    result = jnp.where(
        core == 0,
        jnp.concatenate([kept, incoming], axis=1),
        jnp.concatenate([incoming, kept], axis=1),
    )
    return result.reshape(1, ROWS, 2048)


def solution(mesh):
    split = Mesh(mesh.devices.reshape(4, 4, 4, 2), ("y", "z", "x", "core"))
    weight_spec = P(("y", "z", "x", "core"), None)
    in_specs = (
        P("y", ("z", "x", "core"), None),
        weight_spec,
        weight_spec,
        weight_spec,
        weight_spec,
        P(),
        P("y", None),
    )
    out_specs = P("y", ("z", "x", "core"), None)
    return jax.shard_map(
        per_device, mesh=split, in_specs=in_specs, out_specs=out_specs, check_vma=False
    )
```

time: 427 us -> 227 us (0.53)
  waiting for transfers between devices: 222 us -> 107 us
  blocking collectives: 58.4 us -> 0 us
  other arithmetic: 68.1 us -> 23.6 us
  matrix products: 53.7 us -> 36 us
  starting transfers between devices: 0.12 us -> 17.8 us
  Pallas kernels: 0 us -> 15.6 us
  local copies, waits for them, and re-layouts: 6.82 us -> 12.3 us
    all_gather x4 -> x1, waiting for transfers between devices: 220 us -> 91.9 us  [per_device(): weights = lax.all_gather(block, ('y', 'z', 'x'), axis=0, tiled=True)]
    all_gather x2 -> x0, blocking collectives: 58.4 us -> none  [the longest x1 37.3 us: per_device(): lax.all_gather(w_gates, ('dp', 'ctx'), axis=0, tiled=True)]
    select_n x31 -> x3, other arithmetic: 58.9 us -> 3.13 us  [the longest x1 2.03 us: per_device(): jnp.where(core == 0, jnp.concatenate([kept, incoming], axis=1), jnp.conca...]
    ppermute x0 -> x12, starting transfers between devices: none -> 17.8 us  [the longest x9 14.6 us: shift(): return lax.ppermute(value, axis, [(i, (i + by) % 4) for i in range(4)])]
    dot_general x7 -> x2, matrix products: 53.7 us -> 36 us  [the longest x1 28.9 us: per_device(): jnp.dot(normed, weights[:, :2048], preferred_element_type=F32).astype(BF)]
    pallas_call x0 -> x4, Pallas kernels: none -> 15.6 us  [the longest x1 5.81 us: intra(): pl.pallas_call(intra_kernel, grid=(2, 2), in_specs=[pl.BlockSpec((1, ROWS...]
    ppermute x0 -> x12, waiting for transfers between devices: none -> 14.8 us  [the longest x9 8.46 us: shift(): return lax.ppermute(value, axis, [(i, (i + by) % 4) for i in range(4)])]
    another operation x5 -> x16, other arithmetic: 2.47 us -> 7.67 us  [the longest x5 3.7 us: in_order(): stacked = jnp.stack(blocks)]
  transfers between devices with their start and end apart: 4 -> 13, of which waited for: 4 -> 8; matrix products, arithmetic and copies ran while one was open for 14% -> 6% of each run, Pallas kernels for 0% -> 4%
where the time goes in v1:
time: 227 us; the launch traced here: 226 us
  waiting for transfers between devices  107 us (47%)
  matrix products  36 us (16%)
  other arithmetic  23.6 us (10%)
  starting transfers between devices  17.8 us (8%)
  Pallas kernels  15.6 us (7%)
  between operations  13.7 us (6%)
  local copies, waits for them, and re-layouts  12.3 us (5%)
    all_gather x1, waiting for transfers between devices, per_device(): weights = lax.all_gather(block, ('y', 'z', 'x'), axis=0, tiled=True)  91.9 us
    dot_general x1, matrix products, per_device(): jnp.dot(normed, weights[:, :2048], preferred_element_type=F32).astype(BF)  28.9 us
    ppermute x9, starting transfers between devices, shift(): return lax.ppermute(value, axis, [(i, (i + by) % 4) for i in range(4)])  14.6 us
    ppermute x9, waiting for transfers between devices, shift(): return lax.ppermute(value, axis, [(i, (i + by) % 4) for i in range(4)])  8.46 us
    dot_general x1, matrix products, per_device(): gates = jnp.dot(normed, weights[:, 2048:], preferred_element_type=F32)  7.07 us
    ppermute x3, waiting for transfers between devices, swap(): return lax.ppermute(value, 'core', [(0, 1), (1, 0)])  6.39 us
    pallas_call x1, Pallas kernels, intra(): pl.pallas_call(intra_kernel, grid=(2, 2), in_specs=[pl.BlockSpec((1, ROWS...  5.81 us
    pallas_call x2, Pallas kernels, readout(): pl.pallas_call(readout_kernel, grid=(2,), in_specs=[pl.BlockSpec((1, ROWS...  5.11 us
  transfers between devices with their start and end apart: 13, of which 8 were waited for; matrix products, arithmetic and copies ran while one was open for 6% of the time, Pallas kernels for 4%

profile of v1, /device:TPU:25, one launch (start us, length us, event | category | flops | bytes accessed | tf_op | source)
XLA Modules:
  0.0 225.6 jit_solution(7667718839578873356)
XLA Ops:
  6.5 0.7 constant_dynamic-slice_fusion.8
  7.3 0.9 constant_dynamic-slice_fusion.9
  8.2 0.8 constant_dynamic-slice_fusion.10
  9.1 0.8 collective-permute-start.1
  9.9 0.9 collective-permute-done.1
  10.8 0.8 maximum_select_fusion.1
  11.6 3.7 %fusion.2 = f32[640]{0:T(1024)S(1)} fusion(bf16[1,640,4096]{2,1,0:T(8,128)(2,1)} %param.7), kind=kLoop, calls=%fused_computation.4 | loop fusion | flops 7863680 | bytes 5245440 | tf_op jit(solution)/shard_map/reduce_sum | solution.py:28
  15.4 0.3 copy-done.1
  15.7 4.5 %fusion.3 = bf16[640,4096]{1,0:T(8,128)(2,1)} fusion(bf16[1,640,4096]{2,1,0:T(8,128)(2,1)S(1)} %copy-done.1, f32[640]{0:T(1024)S(1)} %add_rsqrt_fusion), kind=kLoop, calls=%fused_computation.5 | loop fusion | flops 7864320 | bytes 10488320 | tf_op jit(solution)/shard_map/convert_element_type | solution.py:29
  20.2 0.4 collective-permute-start
  21.0 0.6 reduce-window.31
  22.1 1.1 copy.104
  23.8 5.4 %collective-permute-done = bf16[640,4096]{1,0:T(8,128)(2,1)} collective-permute-done((bf16[640,4096]{1,0:T(8,128)(2,1)}, bf16[640,4096]{1,0:T(8,128)(2,1)}, u32[]{:S(2)}, u32[]{:S(2)}) %collective-permute-start) | collective-permute-done | bytes 5242912 | tf_op jit(solution)/shard_map/ppermute | solution.py:19
  29.2 91.9 %all-gather.2.cloned.1.call-done = bf16[4096,2176]{1,0:T(8,128)(2,1)} async-done(((bf16[64,2176]{1,0:T(8,128)(2,1)}), bf16[4096,2176]{1,0:T(8,128)(2,1)}) %all-gather.2.cloned.1.call-update) | async-done | bytes 17825808 | tf_op jit(solution)/shard_map/all_gather | solution.py:210
  121.0 7.1 %fusion.7 = f32[1280,4]{0,1:T(4,128)S(1)} fusion(bf16[640,4096]{1,0:T(8,128)(2,1)} %collective-permute-done, bf16[640,4096]{1,0:T(8,128)(2,1)} %fusion.3, bf16[4096,2176]{1,0:T(8,128)(2,1)} %all-gather.2.cloned.1.call-done), kind=kOutput, calls=%fused_computation.8 | convolution fusion | flops 62914560 | bytes 11554816 | tf_op jit(solution)/shard_map/dot_general | solution.py:215
  128.4 0.5 fusion.11
  128.9 0.3 copy.113
  129.2 1.1 reduce-window.21
  130.5 0.3 reduce-window.24
  131.2 1.4 fusion.56
  132.6 2.0 concatenate.69.cols_ref
  134.7 28.9 %fusion.4.query_ref.key_ref.value_ref = bf16[1280,2048]{1,0:T(8,128)(2,1)} fusion(bf16[4096,2176]{1,0:T(8,128)(2,1)} %all-gather.2.cloned.1.call-done, bf16[640,4096]{1,0:T(8,128)(2,1)} %collective-permute-done, bf16[640,4096]{1,0:T(8,128)(2,1)} %fusion.3), kind=kOutput, calls=%fused_computation.7 | convolution fusion | flops 21498429440 | bytes 32505856 | tf_op jit(solution)/shard_map/dot_general | solution.py:214
  163.6 4.7 %states.1 = bf16[2,2,256,512]{3,2,1,0:T(8,128)(2,1)S(1)} custom-call(f32[2,640,8]{2,1,0:T(8,128)S(1)} %concatenate.69.cols_ref, bf16[1280,2048]{1,0:T(8,128)(2,1)} %fusion.4.query_ref.key_ref.value_ref, bf16[1280,2048]{1,0:T(8,128)(2,1)} %fusion.4.query_ref.key_ref.value_ref), custom_call_target="tpu_custom_call" | custom-call | flops 671088640 | bytes 5242880 | tf_op jit(solution)/shard_map/states/pallas_call | solution.py:42
  168.9 0.7 fusion.26
  169.6 1.1 collective-permute-start.2
  170.8 2.4 %collective-permute-start.3 = (bf16[2,72,512]{2,1,0:T(8,128)(2,1)S(1)}, bf16[2,72,512]{2,1,0:T(8,128)(2,1)}, u32[]{:S(2)}, u32[]{:S(2)}) collective-permute-start(bf16[2,72,512]{2,1,0:T(8,128)(2,1)S(1)} %get-tuple-element.59), channel_id=1, source_target_pairs={{0,4},{2,6},{4,0},{6,2},{1,5},{3,7},{5,1},{7,3},{8,12},{10,14},{12... | collective-permute-start | bytes 442376 | tf_op jit(solution)/shard_map/ppermute | solution.py:23
  173.2 1.2 collective-permute-start.4
  174.4 1.5 collective-permute-done.2
  175.9 4.0 %collective-permute-done.3 = bf16[2,72,512]{2,1,0:T(8,128)(2,1)} collective-permute-done((bf16[2,72,512]{2,1,0:T(8,128)(2,1)S(1)}, bf16[2,72,512]{2,1,0:T(8,128)(2,1)}, u32[]{:S(2)}, u32[]{:S(2)}) %collective-permute-start.3) | collective-permute-done | bytes 147488 | tf_op jit(solution)/shard_map/ppermute | solution.py:23
  179.9 1.1 pad_maximum_fusion.3
  181.4 0.8 fusion.21
  182.3 0.7 fusion.50
  183.2 2.8 %collective-permute-start.6 = (bf16[2,72,512]{2,1,0:T(8,128)(2,1)}, bf16[2,72,512]{2,1,0:T(8,128)(2,1)}, u32[]{:S(2)}, u32[]{:S(2)}) collective-permute-start(bf16[2,72,512]{2,1,0:T(8,128)(2,1)} %get-tuple-element.48), channel_id=1, source_target_pairs={{0,16},{8,24},{16,0},{24,8},{1,17},{9,25},{17,1},{25,9},{2,18},{10... | collective-permute-start | bytes 442376 | tf_op jit(solution)/shard_map/ppermute | solution.py:23
  186.0 1.0 collective-permute-start.7
  187.5 1.3 copy.106
  188.9 2.5 %collective-permute-done.6 = bf16[2,72,512]{2,1,0:T(8,128)(2,1)} collective-permute-done((bf16[2,72,512]{2,1,0:T(8,128)(2,1)}, bf16[2,72,512]{2,1,0:T(8,128)(2,1)}, u32[]{:S(2)}, u32[]{:S(2)}) %collective-permute-start.6) | collective-permute-done | bytes 147488 | tf_op jit(solution)/shard_map/ppermute | solution.py:23
  191.4 0.4 collective-permute-done.7
  191.8 1.1 pad_maximum_fusion.4
  193.6 1.1 fusion.30
  194.9 2.0 collective-permute-start.8
  196.9 3.8 %collective-permute-start.9 = (bf16[2,64,512]{2,1,0:T(8,128)(2,1)S(1)}, bf16[2,64,512]{2,1,0:T(8,128)(2,1)S(1)}, u32[]{:S(2)}, u32[]{:S(2)}) collective-permute-start(bf16[2,64,512]{2,1,0:T(8,128)(2,1)S(1)} %get-tuple-element.39), channel_id=1, source_target_pairs={{0,4},{2,6},{4,0},{6,2},{1,5},{3,7},{5,1},{7,3},{8,12},{10,14},{12... | collective-permute-start | bytes 393224 | tf_op jit(solution)/shard_map/ppermute | solution.py:23
  200.8 5.8 %intra.1.intra_ref = f32[1280,1024]{1,0:T(8,128)S(1)} custom-call(f32[2,640,8]{2,1,0:T(8,128)S(1)} %concatenate.69.cols_ref, f32[2,8,640]{2,1,0:T(8,128)S(1)} %bitcast.126, bf16[1280,2048]{1,0:T(8,128)(2,1)} %fusion.4.query_ref.key_ref.value_ref, bf16[1280,2048]{1,0:T(8,128)(2,1)} %fusion.4.query_ref.key_ref.value_ref, ...), custom_call_target="tpu_custom_call" | custom-call | flops 2516582400 | bytes 12582912 | tf_op jit(solution)/shard_map/intra/pallas_call | solution.py:86
  206.6 2.3 %copy-done = f32[1280,1024]{1,0:T(8,128)} copy-done((f32[1280,1024]{1,0:T(8,128)}, f32[1280,1024]{1,0:T(8,128)S(1)}, u32[]{:S(2)}) %copy-start) | copy-done | bytes 5242904
  209.2 0.3 bitcast_select_fusion.1
  209.5 2.6 %readout.3 = bf16[640,1024]{1,0:T(8,128)(2,1)S(1)} custom-call(f32[2,640,8]{2,1,0:T(8,128)S(1)} %concatenate.69.cols_ref, bf16[1280,2048]{1,0:T(8,128)(2,1)} %fusion.4.query_ref.key_ref.value_ref, f32[1280,1024]{1,0:T(8,128)} %copy-done, bf16[2,256,512]{2,1,0:T(8,128)(2,1)S(1)} %get-tuple-element.19.carried_ref), custom_call_target="tpu_custom_call" | custom-call | flops 335544320 | bytes 5242880 | tf_op jit(solution)/shard_map/readout/pallas_call | solution.py:118
  212.1 2.0 collective-permute-start.11
  214.1 2.5 %readout.2 = bf16[640,1024]{1,0:T(8,128)(2,1)S(1)} custom-call(f32[2,640,8]{2,1,0:T(8,128)S(1)} %concatenate.69.cols_ref, bf16[1280,2048]{1,0:T(8,128)(2,1)} %fusion.4.query_ref.key_ref.value_ref, f32[1280,1024]{1,0:T(8,128)} %copy-done, bf16[2,256,512]{2,1,0:T(8,128)(2,1)S(1)} %get-tuple-element.18.carried_ref), custom_call_target="tpu_custom_call" | custom-call | flops 335544320 | bytes 5242880 | tf_op jit(solution)/shard_map/readout/pallas_call | solution.py:118
  216.8 2.0 maximum_select_fusion
  (74 shorter events, 5.5 us)
Async XLA Ops:
  6.5 114.5 %all-gather.2.cloned.1.call-start = ((), (), s32[]{:S(2)}) async-start(), calls=%async_computation | async-start | bytes 18104320 | tf_op jit(solution)/shard_map/all_gather | solution.py:210
  9.1 1.8 collective-permute-start.1
  11.6 4.0 %copy-start.1 = (bf16[1,640,4096]{2,1,0:T(8,128)(2,1)S(1)}, bf16[1,640,4096]{2,1,0:T(8,128)(2,1)}, u32[]{:S(2)}) copy-start(bf16[1,640,4096]{2,1,0:T(8,128)(2,1)} %param.7) | copy-start | bytes 15728644
  15.7 4.9 %copy-start.2 = (s32[1,16]{1,0:T(1,128)S(1)}, s32[1,16]{1,0:T(1,128)}, u32[]{:S(2)}) copy-start(s32[1,16]{1,0:T(1,128)} %param.13) | copy-start | bytes 196
  15.7 7.6 %copy-start.3 = (f32[4]{0:T(128)S(1)}, f32[4]{0:T(128)}, u32[]{:S(2)}) copy-start(f32[4]{0:T(128)} %param.12) | copy-start | bytes 52
  20.2 9.0 %collective-permute-start = (bf16[640,4096]{1,0:T(8,128)(2,1)}, bf16[640,4096]{1,0:T(8,128)(2,1)}, u32[]{:S(2)}, u32[]{:S(2)}) collective-permute-start(bf16[640,4096]{1,0:T(8,128)(2,1)} %fusion.3), channel_id=1, source_target_pairs={{0,1},{1,0},{2,3},{3,2},{4,5},{5,4},{6,7},{7,6},{8,9},{9,8},{10,11... | collective-permute-start | bytes 15728648 | tf_op jit(solution)/shard_map/ppermute | solution.py:19
  169.6 6.2 %collective-permute-start.2 = (bf16[2,72,512]{2,1,0:T(8,128)(2,1)}, bf16[2,72,512]{2,1,0:T(8,128)(2,1)}, u32[]{:S(2)}, u32[]{:S(2)}) collective-permute-start(bf16[2,72,512]{2,1,0:T(8,128)(2,1)} %get-tuple-element.58), channel_id=1, source_target_pairs={{0,2},{2,4},{4,6},{6,0},{1,3},{3,5},{5,7},{7,1},{8,10},{10,12},{12... | collective-permute-start | bytes 442376 | tf_op jit(solution)/shard_map/ppermute | solution.py:23
  170.8 9.1 %collective-permute-start.3 = (bf16[2,72,512]{2,1,0:T(8,128)(2,1)S(1)}, bf16[2,72,512]{2,1,0:T(8,128)(2,1)}, u32[]{:S(2)}, u32[]{:S(2)}) collective-permute-start(bf16[2,72,512]{2,1,0:T(8,128)(2,1)S(1)} %get-tuple-element.59), channel_id=1, source_target_pairs={{0,4},{2,6},{4,0},{6,2},{1,5},{3,7},{5,1},{7,3},{8,12},{10,14},{12... | collective-permute-start | bytes 442376 | tf_op jit(solution)/shard_map/ppermute | solution.py:23
  173.2 6.7 %collective-permute-start.4 = (bf16[2,72,512]{2,1,0:T(8,128)(2,1)S(1)}, bf16[2,72,512]{2,1,0:T(8,128)(2,1)}, u32[]{:S(2)}, u32[]{:S(2)}) collective-permute-start(bf16[2,72,512]{2,1,0:T(8,128)(2,1)S(1)} %get-tuple-element.60), channel_id=1, source_target_pairs={{0,6},{2,0},{4,2},{6,4},{1,7},{3,1},{5,3},{7,5},{8,14},{10,8},{12,... | collective-permute-start | bytes 442376 | tf_op jit(solution)/shard_map/ppermute | solution.py:23
  183.0 5.8 %collective-permute-start.5 = (bf16[2,72,512]{2,1,0:T(8,128)(2,1)}, bf16[2,72,512]{2,1,0:T(8,128)(2,1)}, u32[]{:S(2)}, u32[]{:S(2)}) collective-permute-start(bf16[2,72,512]{2,1,0:T(8,128)(2,1)} %get-tuple-element.48), channel_id=1, source_target_pairs={{0,8},{8,16},{16,24},{24,0},{1,9},{9,17},{17,25},{25,1},{2,10},{10... | collective-permute-start | bytes 442376 | tf_op jit(solution)/shard_map/ppermute | solution.py:23
  183.2 8.2 %collective-permute-start.6 = (bf16[2,72,512]{2,1,0:T(8,128)(2,1)}, bf16[2,72,512]{2,1,0:T(8,128)(2,1)}, u32[]{:S(2)}, u32[]{:S(2)}) collective-permute-start(bf16[2,72,512]{2,1,0:T(8,128)(2,1)} %get-tuple-element.48), channel_id=1, source_target_pairs={{0,16},{8,24},{16,0},{24,8},{1,17},{9,25},{17,1},{25,9},{2,18},{10... | collective-permute-start | bytes 442376 | tf_op jit(solution)/shard_map/ppermute | solution.py:23
  186.0 5.8 %collective-permute-start.7 = (bf16[2,72,512]{2,1,0:T(8,128)(2,1)}, bf16[2,72,512]{2,1,0:T(8,128)(2,1)}, u32[]{:S(2)}, u32[]{:S(2)}) collective-permute-start(bf16[2,72,512]{2,1,0:T(8,128)(2,1)} %get-tuple-element.48), channel_id=1, source_target_pairs={{0,24},{8,0},{16,8},{24,16},{1,25},{9,1},{17,9},{25,17},{2,26},{10... | collective-permute-start | bytes 442376 | tf_op jit(solution)/shard_map/ppermute | solution.py:23
  194.9 14.0 %collective-permute-start.8 = (bf16[2,64,512]{2,1,0:T(8,128)(2,1)S(1)}, bf16[2,64,512]{2,1,0:T(8,128)(2,1)S(1)}, u32[]{:S(2)}, u32[]{:S(2)}) collective-permute-start(bf16[2,64,512]{2,1,0:T(8,128)(2,1)S(1)} %get-tuple-element.40), channel_id=1, source_target_pairs={{0,2},{2,4},{4,6},{6,0},{1,3},{3,5},{5,7},{7,1},{8,10},{10,12},{12... | collective-permute-start | bytes 393224 | tf_op jit(solution)/shard_map/ppermute | solution.py:23
  196.9 12.0 %collective-permute-start.9 = (bf16[2,64,512]{2,1,0:T(8,128)(2,1)S(1)}, bf16[2,64,512]{2,1,0:T(8,128)(2,1)S(1)}, u32[]{:S(2)}, u32[]{:S(2)}) collective-permute-start(bf16[2,64,512]{2,1,0:T(8,128)(2,1)S(1)} %get-tuple-element.39), channel_id=1, source_target_pairs={{0,4},{2,6},{4,0},{6,2},{1,5},{3,7},{5,1},{7,3},{8,12},{10,14},{12... | collective-permute-start | bytes 393224 | tf_op jit(solution)/shard_map/ppermute | solution.py:23
  200.8 8.1 %collective-permute-start.10 = (bf16[2,64,512]{2,1,0:T(8,128)(2,1)S(1)}, bf16[2,64,512]{2,1,0:T(8,128)(2,1)S(1)}, u32[]{:S(2)}, u32[]{:S(2)}) collective-permute-start(bf16[2,64,512]{2,1,0:T(8,128)(2,1)S(1)} %get-tuple-element.38), channel_id=1, source_target_pairs={{0,6},{2,0},{4,2},{6,4},{1,7},{3,1},{5,3},{7,5},{8,14},{10,8},{12,... | collective-permute-start | bytes 393224 | tf_op jit(solution)/shard_map/ppermute | solution.py:23
  206.6 2.3 %copy-start = (f32[1280,1024]{1,0:T(8,128)}, f32[1280,1024]{1,0:T(8,128)S(1)}, u32[]{:S(2)}) copy-start(f32[1280,1024]{1,0:T(8,128)S(1)} %intra.1.intra_ref) | copy-start | bytes 15728644
  212.1 4.7 %collective-permute-start.11 = (bf16[640,1024]{1,0:T(8,128)(2,1)S(1)}, bf16[640,1024]{1,0:T(8,128)(2,1)S(1)}, u32[]{:S(2)}, u32[]{:S(2)}) collective-permute-start(bf16[640,1024]{1,0:T(8,128)(2,1)S(1)} %readout.3), channel_id=1, source_target_pairs={{0,1},{1,0},{2,3},{3,2},{4,5},{5,4},{6,7},{7,6},{8,9},{9,8},{10,11... | collective-permute-start | bytes 3932168 | tf_op jit(solution)/shard_map/ppermute | solution.py:19
Sparse Core Ops, SparseCore 0:
  11.7 109.2 all-gather.1

commit v2 on v1

v2 whole, which is shorter than its diff:
```python
import functools
import itertools

import jax
import jax.numpy as jnp
from jax import lax
from jax.experimental import pallas as pl
from jax.experimental.pallas import tpu as pltpu
from jax.sharding import Mesh, PartitionSpec as P

ROWS = 640
DQK = 256
DV = 512
OWN = 32
PIECE = 64
EXTRA = 16
WIDE = 512
BF = jnp.bfloat16
F32 = jnp.float32
COST = pl.CostEstimate(flops=0, bytes_accessed=1 << 10, transcendentals=0)
SMALL = pltpu.CompilerParams(vmem_limit_bytes=24 * 1024 * 1024)
PARAMS = pltpu.CompilerParams(vmem_limit_bytes=60 * 1024 * 1024)


def swap(value):
    return lax.ppermute(value, "core", [(0, 1), (1, 0)])


def shift(value, axis, by):
    return lax.ppermute(value, axis, [(i, (i + by) % 4) for i in range(4)])


def hop(value, axes, by):
    names, pairs = ("y", "z", "x", "core"), []
    for source in itertools.product(range(4), range(4), range(4), range(2)):
        target = list(source)
        at = names.index(axes[source[3]])
        target[at] = (target[at] + by) % 4
        flat = [((p[0] * 4 + p[1]) * 4 + p[2]) * 2 + p[3] for p in (source, target)]
        pairs.append(tuple(flat))
    return lax.ppermute(value, names, pairs)


def around(value, axes):
    return (value,) + tuple(hop(value, axes, by) for by in (3, 2, 1))


def places(at):
    return jnp.stack([at, (at + 1) % 4, (at + 2) % 4, (at + 3) % 4]).astype(jnp.int32)


def normalize_kernel(own_ref, mate_ref, out_ref):
    raw = jnp.where(pl.program_id(0) == 0, own_ref[...], mate_ref[...])
    values = raw.astype(F32)
    scale = lax.rsqrt(jnp.mean(values * values, axis=-1, keepdims=True) + 1e-06)
    out_ref[...] = (values * scale).astype(BF)


def normalize(own, mate):
    tile = 128
    steps = ROWS // tile
    return pl.pallas_call(
        normalize_kernel,
        grid=(2, steps),
        in_specs=[
            pl.BlockSpec((tile, 4096), lambda s, i: (jnp.where(s == 0, i, steps - 1), 0)),
            pl.BlockSpec((tile, 4096), lambda s, i: (jnp.where(s == 0, 0, i), 0)),
        ],
        out_specs=pl.BlockSpec((tile, 4096), lambda s, i: (s * steps + i, 0)),
        out_shape=jax.ShapeDtypeStruct((2 * ROWS, 4096), BF),
        compiler_params=PARAMS,
        cost_estimate=pl.CostEstimate(flops=0, bytes_accessed=21 << 20, transcendentals=0),
        name="normalize",
    )(own, mate)


def prepare_kernel(
    core_ref, query, key, value, mate_query, mate_key, mate_value, region, held_ref, rest_ref
):
    core = core_ref[0]
    narrow = pl.ds(pl.multiple_of(core * WIDE, WIDE), WIDE)
    wide = pl.ds(pl.multiple_of(core * 2 * WIDE, WIDE), 2 * WIDE)
    for source, rows in (((query, key, value), core), ((mate_query, mate_key, mate_value), 1 - core)):
        rows = pl.ds(pl.multiple_of(rows * OWN, OWN), OWN)
        held_ref[rows, :] = source[0][:, narrow]
        rest_ref[rows, :WIDE] = source[1][:, narrow]
        rest_ref[rows, WIDE:] = source[2][:, wide]
    held_ref[PIECE:, :] = region[...]


def prepare(core, own, mate, region):
    vmem = pl.BlockSpec(memory_space=pltpu.VMEM)
    return pl.pallas_call(
        prepare_kernel,
        in_specs=[pl.BlockSpec(memory_space=pltpu.SMEM)] + [vmem] * 7,
        out_specs=[vmem] * 2,
        out_shape=[
            jax.ShapeDtypeStruct((PIECE + EXTRA, WIDE), BF),
            jax.ShapeDtypeStruct((PIECE, 3 * WIDE), BF),
        ],
        compiler_params=PARAMS,
        cost_estimate=COST,
        name="prepare",
    )(core, *own, *mate, region)


def assemble_kernel(rows, final, places, *refs):
    blocks, out, held, regions, sems_in, sems_more, sems_out = refs[:4], refs[4:-5], *refs[-5:]
    loads, extras = [], []
    for which, block in enumerate(blocks):
        start = pl.multiple_of(places[which] * rows, PIECE)
        loads.append(
            pltpu.make_async_copy(
                block.at[pl.ds(0, rows), :], held.at[pl.ds(start, rows), :], sems_in.at[which]
            )
        )
        extras.append(
            pltpu.make_async_copy(
                block.at[pl.ds(rows, EXTRA), :], regions.at[which], sems_more.at[which]
            )
        )
    for copy in extras + loads:
        copy.start()
    for copy in extras:
        copy.wait()
    held[4 * rows :, :] = (regions[0] + regions[1]) + (regions[2] + regions[3])
    for copy in loads:
        copy.wait()
    if final:
        stores = [
            pltpu.make_async_copy(held.at[pl.ds(0, 4 * rows), :], out[0], sems_out.at[0]),
            pltpu.make_async_copy(held.at[pl.ds(4 * rows, EXTRA), :], out[1], sems_out.at[1]),
        ]
    else:
        stores = [pltpu.make_async_copy(held, out[0], sems_out.at[0])]
    for copy in stores:
        copy.start()
    for copy in stores:
        copy.wait()


def assemble(places, blocks, rows, final):
    hbm = pl.BlockSpec(memory_space=pl.ANY)
    if final:
        shapes = [(4 * rows, WIDE), (EXTRA, WIDE)]
    else:
        shapes = [(4 * rows + EXTRA, WIDE)]
    return pl.pallas_call(
        functools.partial(assemble_kernel, rows, final),
        in_specs=[pl.BlockSpec(memory_space=pltpu.SMEM)] + [hbm] * 4,
        out_specs=[hbm] * len(shapes),
        out_shape=[jax.ShapeDtypeStruct(shape, BF) for shape in shapes],
        scratch_shapes=[
            pltpu.VMEM((4 * rows + EXTRA, WIDE), BF),
            pltpu.VMEM((4, EXTRA, WIDE), BF),
            pltpu.SemaphoreType.DMA((4,)),
            pltpu.SemaphoreType.DMA((4,)),
            pltpu.SemaphoreType.DMA((2,)),
        ],
        compiler_params=PARAMS,
        cost_estimate=COST,
        name="assemble",
    )(places, *blocks)


def restore_kernel(places, *refs):
    blocks, out, held, sems_in, sem_out = refs[:4], *refs[4:]

    def run(target):
        copies = []
        for which, block in enumerate(blocks):
            for y in range(4):
                copies.append(
                    pltpu.make_async_copy(
                        block.at[:, y], target(y, places[which]), sems_in.at[4 * which + y]
                    )
                )
        for copy in copies:
            copy.start()
        for copy in copies:
            copy.wait()

    pl.when(places[4] == 0)(lambda: run(lambda y, x: held.at[y, :, x]))
    pl.when(places[4] == 1)(lambda: run(lambda y, z: held.at[y, z]))
    store = pltpu.make_async_copy(held, out, sem_out)
    store.start()
    store.wait()


def restore(places, blocks):
    hbm = pl.BlockSpec(memory_space=pl.ANY)
    shape = (4, 4, 4, PIECE, WIDE)
    return pl.pallas_call(
        restore_kernel,
        in_specs=[pl.BlockSpec(memory_space=pltpu.SMEM)] + [hbm] * 4,
        out_specs=hbm,
        out_shape=jax.ShapeDtypeStruct(shape, BF),
        scratch_shapes=[
            pltpu.VMEM(shape, BF),
            pltpu.SemaphoreType.DMA((16,)),
            pltpu.SemaphoreType.DMA,
        ],
        compiler_params=PARAMS,
        cost_estimate=COST,
        name="restore",
    )(places, *(block.reshape(4, 4, PIECE, WIDE) for block in blocks)).reshape(4096, WIDE)


def together(*values):
    return lax.optimization_barrier(values)


def state_kernel(cols_ref, key_ref, left_ref, right_ref, out_ref):
    for head, value_ref in enumerate((left_ref, right_ref)):
        weight = cols_ref[0, :, 4 + head : 5 + head]
        keys = key_ref[:, head * DQK : (head + 1) * DQK]
        scaled = (keys.astype(F32) * weight).astype(BF)
        out_ref[0, head] = lax.dot_general(
            scaled, value_ref[...], (((0,), (0,)), ((), ())), preferred_element_type=F32
        ).astype(BF)


def states(cols, held):
    parts = [pl.BlockSpec((ROWS, WIDE), lambda s, n=n: (s, n)) for n in range(3)]
    return pl.pallas_call(
        state_kernel,
        grid=(2,),
        in_specs=[pl.BlockSpec((1, ROWS, 8), lambda s: (s, 0, 0)), *parts],
        out_specs=pl.BlockSpec((1, 2, DQK, DV), lambda s: (s, 0, 0, 0)),
        out_shape=jax.ShapeDtypeStruct((2, 2, DQK, DV), BF),
        compiler_params=SMALL,
        cost_estimate=COST,
        name="states",
    )(cols, held, held, held)


def intra_kernel(cols_ref, rows_ref, query_ref, key_ref, left_ref, right_ref, out_ref):
    segment = cols_ref[0, :, 6:7]
    segment_row = rows_ref[0, 4:5, :]
    for head, value_ref in enumerate((left_ref, right_ref)):
        cumul = cols_ref[0, :, head : head + 1]
        cumul_row = rows_ref[0, head : head + 1, :]
        gate_row = rows_ref[0, 2 + head : 3 + head, :]
        features = slice(head * DQK, (head + 1) * DQK)
        for start, size in ((0, 256), (256, 384)):
            reach = start + size
            scores = lax.dot_general(
                query_ref[start:reach, features],
                key_ref[:reach, features],
                (((1,), (1,)), ((), ())),
                preferred_element_type=F32,
            ) * (DQK**-0.5)
            later = start + lax.broadcasted_iota(jnp.int32, (size, reach), 0)
            earlier = lax.broadcasted_iota(jnp.int32, (size, reach), 1)
            keep = (later >= earlier) & (segment[start:reach] == segment_row[:, :reach])
            diff = cumul[start:reach] - cumul_row[:, :reach] + gate_row[:, :reach]
            mixed = (scores * jnp.exp(jnp.where(keep, diff, -1e30))).astype(BF)
            out_ref[start:reach, head * DV : (head + 1) * DV] = jnp.dot(
                mixed, value_ref[:reach, :], preferred_element_type=F32
            )


def intra(cols, rows, query, held):
    parts = [pl.BlockSpec((ROWS, WIDE), lambda s, n=n: (s, n)) for n in (0, 0, 1, 2)]
    return pl.pallas_call(
        intra_kernel,
        grid=(2,),
        in_specs=[
            pl.BlockSpec((1, ROWS, 8), lambda s: (s, 0, 0)),
            pl.BlockSpec((1, 8, ROWS), lambda s: (s, 0, 0)),
            *parts,
        ],
        out_specs=pl.BlockSpec((ROWS, 2 * DV), lambda s: (s, 0)),
        out_shape=jax.ShapeDtypeStruct((2 * ROWS, 2 * DV), F32),
        compiler_params=SMALL,
        cost_estimate=COST,
        name="intra",
    )(cols, rows, query, held, held, held)


def readout_kernel(cols_ref, query_ref, intra_ref, carried_ref, out_ref):
    head = pl.program_id(0)
    reach = jnp.where(head == 0, cols_ref[0, :, 2:3], cols_ref[0, :, 3:4])
    between = jnp.dot(query_ref[...], carried_ref[0], preferred_element_type=F32) * reach
    readout = intra_ref[...] + between
    scale = lax.rsqrt(jnp.mean(readout * readout, axis=-1, keepdims=True) + 1e-05)
    out_ref[...] = (readout * scale).astype(BF)


def readout(slot, cols, qkv, inner, carried):
    return pl.pallas_call(
        readout_kernel,
        grid=(2,),
        in_specs=[
            pl.BlockSpec((1, ROWS, 8), lambda h: (slot, 0, 0)),
            pl.BlockSpec((ROWS, DQK), lambda h: (slot, h)),
            pl.BlockSpec((ROWS, DV), lambda h: (slot, h)),
            pl.BlockSpec((1, DQK, DV), lambda h: (h, 0, 0)),
        ],
        out_specs=pl.BlockSpec((ROWS, DV), lambda h: (0, h)),
        out_shape=jax.ShapeDtypeStruct((ROWS, 2 * DV), BF),
        compiler_params=SMALL,
        cost_estimate=COST,
        name="readout",
    )(cols, qkv, inner, carried)


def join(decay, earlier, later):
    return (decay.astype(F32)[:, None, None] * earlier.astype(F32) + later.astype(F32)).astype(BF)


def times(left, right):
    return (left.astype(F32) * right.astype(F32)).astype(BF)


def pack(state, decay):
    tail = jnp.broadcast_to(decay[:, None, None], (2, 8, DV))
    return jnp.concatenate([state, tail], axis=1)


def unpack(message):
    return message[:, :-8], message[:, -1, 0]


def in_order(mine, axis, send):
    place = lax.axis_index(axis)
    blocks = [mine] + [shift(send(by), axis, by) for by in (1, 2, 3)]
    stacked = jnp.stack(blocks)
    return [lax.dynamic_index_in_dim(stacked, (place - j) % 4, 0, False) for j in range(4)]


def carry_in(decay, state, query, more):
    x, z = lax.axis_index("x"), lax.axis_index("z")
    quarters = state.reshape(2, 4, DQK // 4, DV)

    def piece(by):
        return pack(lax.dynamic_index_in_dim(quarters, (x + by) % 4, 1, False), decay)

    line = [unpack(block) for block in in_order(piece(0), "x", piece)]
    prior = jnp.zeros_like(line[0][0])
    reach = jnp.ones_like(decay)
    priors, reaches = [], []
    for block, fade in line:
        priors.append(prior)
        reaches.append(reach)
        prior = join(fade, prior, block)
        reach = times(fade, reach)
    whole, query = together(pack(prior, reach), query)
    before = jnp.zeros_like(prior)
    for j, message in enumerate(in_order(whole, "z", lambda by: whole)):
        block, fade = unpack(message)
        before = jnp.where(j < z, join(fade, before, block), before)
    backs = jnp.stack([join(reaches[j], before, priors[j]) for j in range(4)])
    backs, inner = together(backs, more(query))

    def back(by):
        return lax.dynamic_index_in_dim(backs, (x + by) % 4, 0, False)

    return jnp.stack(in_order(back(0), "x", back), axis=1).reshape(2, DQK, DV), inner


def gate_rows(w_gates, core, place):
    gates = w_gates.T.reshape(2, 2, 2, OWN).transpose(1, 0, 2, 3).reshape(2, 4, OWN)
    mate = swap(gates)
    gates = jnp.where(
        core == 0,
        jnp.concatenate([gates[0], mate[0]], axis=1),
        jnp.concatenate([mate[1], gates[1]], axis=1),
    )
    gates = jnp.pad(gates.reshape(1, 4 * PIECE), ((0, 0), (0, WIDE - 4 * PIECE)))
    row = lax.broadcasted_iota(jnp.int32, (EXTRA, WIDE), 0)
    return jnp.where(row == place, gates, jnp.zeros_like(gates))


def per_device(tokens, w_query, w_key, w_value, w_gates, forget_bias, doc_lengths):
    core = lax.axis_index("core")
    y, z, x = lax.axis_index("y"), lax.axis_index("z"), lax.axis_index("x")
    chip = z * 4 + x
    last, middle = jnp.where(core == 0, x, z), jnp.where(core == 0, z, x)
    core_scalar = core[None].astype(jnp.int32)
    restore_places = jnp.concatenate([places(last), core_scalar])

    own = (w_query, w_key, w_value)
    mate = tuple(swap(weight) for weight in own)
    held, rest = prepare(core_scalar, own, mate, gate_rows(w_gates, core, middle * 4 + y))
    rest = lax.all_gather(rest, ("y", "z", "x"), axis=0, tiled=True)
    tokens = together(tokens[0], held)[0]
    normed = normalize(tokens, swap(tokens))

    (held,) = assemble(places(y), together(*around(held, "yy")), PIECE, False)
    held, region = assemble(places(middle), together(*around(held, "zx")), 4 * PIECE, True)
    regions = jnp.stack(together(*around(region, "xz")))
    regions = jnp.stack([lax.dynamic_index_in_dim(regions, (j - last) % 4, 0, False) for j in range(4)])
    regions = regions[:, :, : 4 * PIECE].reshape(4, 4, 4, 4, PIECE)
    w_gates = jnp.where(
        core == 0, regions.transpose(3, 2, 1, 0, 4), regions.transpose(3, 2, 0, 1, 4)
    ).reshape(4, 4096)
    gates = lax.dot_general(
        normed, w_gates, (((1,), (1,)), ((), ())), preferred_element_type=F32
    )
    held, rest, gates = together(held, rest, gates)
    blocks = around(held, "xz")

    gates = gates.reshape(2, ROWS, 4)
    lengths = doc_lengths[0]
    starts = jnp.cumsum(lengths) - lengths
    shard = chip * 2 + jnp.stack([core, 1 - core])
    positions = shard[:, None] * ROWS + jnp.arange(ROWS, dtype=jnp.int32)[None, :]
    resets = jnp.any(positions[:, :, None] == starts[None, None, :], axis=-1)
    bias = lax.dynamic_slice_in_dim(forget_bias, core * 2, 2)
    in_gate = gates[:, :, :2]
    cumul = jnp.cumsum(jax.nn.log_sigmoid(gates[:, :, 2:] + bias), axis=1)
    segment = jnp.cumsum(resets.astype(jnp.int32), axis=1)
    last = cumul[:, -1]
    same = (segment == segment[:, -1:])[:, :, None]
    weight = jnp.exp(jnp.where(same, last[:, None, :] - cumul + in_gate, -1e30))
    decay = (jnp.exp(last) * (segment[:, -1:] == 0).astype(F32)).astype(BF)
    reach = jnp.exp(cumul) * (segment == 0).astype(F32)[:, :, None] * (DQK**-0.5)
    seg = segment.astype(F32)[:, :, None]
    cols = jnp.concatenate([cumul, reach, weight, seg, jnp.zeros_like(seg)], axis=2)
    rows = jnp.concatenate([cumul, in_gate, seg, jnp.zeros_like(seg), weight], axis=2)
    rows = rows.transpose(0, 2, 1)

    rest, cols, rows, decay, restore_places = together(rest, cols, rows, decay, restore_places)
    held = jnp.dot(normed, rest, preferred_element_type=F32).astype(BF)
    state = states(cols, held)
    *blocks, state = together(*blocks, state)
    w_query = restore(restore_places, blocks)
    query = jnp.dot(normed, w_query, preferred_element_type=F32).astype(BF)
    first = lax.dynamic_index_in_dim(state, core, 0, False)
    second = lax.dynamic_index_in_dim(state, 1 - core, 0, False)
    fade_first = lax.dynamic_index_in_dim(decay, core, 0, False)
    fade_second = lax.dynamic_index_in_dim(decay, 1 - core, 0, False)
    chip_state = join(fade_second, first, second)
    carried, inner = carry_in(
        times(fade_first, fade_second), chip_state, query, lambda query: intra(cols, rows, query, held)
    )
    carried_second = join(fade_first, carried, first)
    mine = jnp.where(core == 0, carried, carried_second)
    other = jnp.where(core == 0, carried_second, carried)
    outgoing = readout(1, cols, query, inner, other)
    incoming = swap(outgoing)
    kept = readout(0, cols, query, inner, mine)
    result = jnp.where(
        core == 0,
        jnp.concatenate([kept, incoming], axis=1),
        jnp.concatenate([incoming, kept], axis=1),
    )
    return result.reshape(1, ROWS, 2048)


def solution(mesh):
    split = Mesh(mesh.devices.reshape(4, 4, 4, 2), ("y", "z", "x", "core"))
    weight_spec = P(("y", "z", "x", "core"), None)
    in_specs = (
        P("y", ("z", "x", "core"), None),
        weight_spec,
        weight_spec,
        weight_spec,
        weight_spec,
        P(),
        P("y", None),
    )
    out_specs = P("y", ("z", "x", "core"), None)
    return jax.shard_map(
        per_device, mesh=split, in_specs=in_specs, out_specs=out_specs, check_vma=False
    )
```

time: 227 us -> 203 us (0.89)
  waiting for transfers between devices: 107 us -> 57.6 us
  Pallas kernels: 15.6 us -> 34.4 us
  starting transfers between devices: 17.8 us -> 31 us
  other arithmetic: 23.6 us -> 13.4 us
  matrix products: 36 us -> 39.6 us
    all_gather x1, waiting for transfers between devices: 91.9 us -> 35.7 us  [per_device(): rest = lax.all_gather(rest, ('y', 'z', 'x'), axis=0, tiled=True)]
    pallas_call x2 -> x7, Pallas kernels: 10.5 us -> 31.7 us  [the longest x1 13.5 us: normalize(): pl.pallas_call(normalize_kernel, grid=(2, steps), in_specs=[pl.BlockSpec(...]
    ppermute x0 -> x12, waiting for transfers between devices: none -> 15.7 us  [hop(): return lax.ppermute(value, names, pairs)]
    ppermute x0 -> x12, starting transfers between devices: none -> 13.7 us  [hop(): return lax.ppermute(value, names, pairs)]
    ppermute x3 -> x6, waiting for transfers between devices: 6.39 us -> 1.88 us  [swap(): return lax.ppermute(value, 'core', [(0, 1), (1, 0)])]
    convert_element_type x1 -> x0, other arithmetic: 4.5 us -> none  [normalize(): return (values * scale).astype(BF)]
    ppermute x9, waiting for transfers between devices: 8.46 us -> 4.29 us  [shift(): return lax.ppermute(value, axis, [(i, (i + by) % 4) for i in range(4)])]
    reduce_sum x1 -> x0, other arithmetic: 3.73 us -> none  [normalize(): scale = lax.rsqrt(jnp.mean(values * values, axis=-1, keepdims=True) + 1e-06)]
  transfers between devices with their start and end apart: 13 -> 28, of which waited for: 8 -> 13; matrix products, arithmetic and copies ran while one was open for 6% -> 25% of each run, Pallas kernels for 4% -> 16%
where the time goes in v2:
time: 203 us; the launch traced here: 201 us
  waiting for transfers between devices  57.6 us (28%)
  matrix products  39.6 us (20%)
  Pallas kernels  34.4 us (17%)
  starting transfers between devices  31 us (15%)
  between operations  14.1 us (7%)
  other arithmetic  13.4 us (7%)
  local copies, waits for them, and re-layouts  10.9 us (5%)
    all_gather x1, waiting for transfers between devices, per_device(): rest = lax.all_gather(rest, ('y', 'z', 'x'), axis=0, tiled=True)  35.7 us
    dot_general x1, matrix products, per_device(): held = jnp.dot(normed, rest, preferred_element_type=F32).astype(BF)  23.2 us
    ppermute x12, waiting for transfers between devices, hop(): return lax.ppermute(value, names, pairs)  15.7 us
    ppermute x12, starting transfers between devices, hop(): return lax.ppermute(value, names, pairs)  13.7 us
    pallas_call x1, Pallas kernels, normalize(): pl.pallas_call(normalize_kernel, grid=(2, steps), in_specs=[pl.BlockSpec(...  13.5 us
    ppermute x9, starting transfers between devices, shift(): return lax.ppermute(value, axis, [(i, (i + by) % 4) for i in range(4)])  11.4 us
    dot_general x1, matrix products, per_device(): query = jnp.dot(normed, w_query, preferred_element_type=F32).astype(BF)  9.52 us
    dot_general x1, matrix products, per_device(): lax.dot_general(normed, w_gates, (((1,), (1,)), ((), ())), preferred_elem...  6.86 us
  transfers between devices with their start and end apart: 28, of which 13 were waited for; matrix products, arithmetic and copies ran while one was open for 25% of the time, Pallas kernels for 16%

profile of v2, /device:TPU:25, one launch (start us, length us, event | category | flops | bytes accessed | tf_op | source)
XLA Modules:
  0.0 201.0 jit_solution(6929368829682986424)
XLA Ops:
  6.5 0.7 copy.100
  7.2 0.7 collective-permute-start.3
  8.9 0.7 broadcast_select_fusion.region
  10.6 1.8 prepare.1
  12.6 0.7 copy.76
  16.6 2.0 collective-permute-start.6
  19.2 2.3 %collective-permute-done.4.refs_1_ = bf16[80,512]{1,0:T(8,128)(2,1)S(1)} collective-permute-done((bf16[80,512]{1,0:T(8,128)(2,1)}, bf16[80,512]{1,0:T(8,128)(2,1)S(1)}, u32[]{:S(2)}, u32[]{:S(2)}) %collective-permute-start.4) | collective-permute-done | bytes 81952 | tf_op jit(solution)/shard_map/ppermute | solution.py:41
  21.6 1.1 collective-permute-done.6.refs_3_
  23.3 2.5 %assemble.2.refs_0_ = bf16[272,512]{1,0:T(8,128)(2,1)} custom-call(s32[4]{0:T(128)} %get-tuple-element.134.places, bf16[80,512]{1,0:T(8,128)(2,1)} %get-tuple-element.40.refs_0_, bf16[80,512]{1,0:T(8,128)(2,1)} %copy-done.8, bf16[80,512]{1,0:T(8,128)(2,1)} %copy-done.9, bf16[80,512]{1,0:T(8,128)(2,1)} %copy-done.10), custom_call_target="tpu_custom_call" | custom-call | bytes 1024 | tf_op jit(solution)/shard_map/assemble/pallas_call | solution.py:148
  25.8 2.5 %collective-permute-start.7 = (bf16[272,512]{1,0:T(8,128)(2,1)}, bf16[272,512]{1,0:T(8,128)(2,1)S(1)}, u32[]{:S(2)}, u32[]{:S(2)}) collective-permute-start(bf16[272,512]{1,0:T(8,128)(2,1)} %assemble.2.refs_0_), channel_id=1, source_target_pairs={{0,24},{1,7},{2,26},{3,1},{4,28},{5,3},{6,30},{7,5},{8,0},{9,15},{... | collective-permute-start | bytes 835592 | tf_op jit(solution)/shard_map/ppermute | solution.py:41
  29.7 6.5 %collective-permute-done.7.refs_1_ = bf16[272,512]{1,0:T(8,128)(2,1)S(1)} collective-permute-done((bf16[272,512]{1,0:T(8,128)(2,1)}, bf16[272,512]{1,0:T(8,128)(2,1)S(1)}, u32[]{:S(2)}, u32[]{:S(2)}) %collective-permute-start.7) | collective-permute-done | bytes 278560 | tf_op jit(solution)/shard_map/ppermute | solution.py:41
  36.6 3.4 %collective-permute-done.9.refs_3_ = bf16[272,512]{1,0:T(8,128)(2,1)S(1)} collective-permute-done((bf16[272,512]{1,0:T(8,128)(2,1)}, bf16[272,512]{1,0:T(8,128)(2,1)S(1)}, u32[]{:S(2)}, u32[]{:S(2)}) %collective-permute-start.9) | collective-permute-done | bytes 278560 | tf_op jit(solution)/shard_map/ppermute | solution.py:41
  40.1 0.7 copy-done.6
  40.8 3.0 %assemble.3 = (bf16[1024,512]{1,0:T(8,128)(2,1)}, bf16[16,512]{1,0:T(8,128)(2,1)}) custom-call(s32[4]{0:T(128)} %get-tuple-element.133.places, bf16[272,512]{1,0:T(8,128)(2,1)} %assemble.2.refs_0_, bf16[272,512]{1,0:T(8,128)(2,1)} %copy-done.4, bf16[272,512]{1,0:T(8,128)(2,1)} %copy-done.5, bf16[272,512]{1,0:T(8,128)(2,1)} %copy-done.6), custom_call_target="tpu_custom_call" | custom-call | bytes 1024 | tf_op jit(solution)/shard_map/assemble/pallas_call | solution.py:148
  43.8 2.8 %collective-permute-start.11 = (bf16[16,512]{1,0:T(8,128)(2,1)}, bf16[16,512]{1,0:T(8,128)(2,1)S(1)}, u32[]{:S(2)}, u32[]{:S(2)}) collective-permute-start(bf16[16,512]{1,0:T(8,128)(2,1)} %get-tuple-element.52), channel_id=1, source_target_pairs={{0,6},{1,25},{2,0},{3,27},{4,2},{5,29},{6,4},{7,31},{8,14},{9,1},{... | collective-permute-start | bytes 49160 | tf_op jit(solution)/shard_map/ppermute | solution.py:41
  46.6 0.7 collective-permute-start.13
  47.7 0.7 dynamic_slice.97
  49.1 1.9 collective-permute-done.12
  51.0 0.7 pad_maximum_fusion.10
  52.1 13.5 %normalize.1 = bf16[1280,4096]{1,0:T(8,128)(2,1)} custom-call(bf16[640,4096]{1,0:T(8,128)(2,1)} %bitcast.159, bf16[640,4096]{1,0:T(8,128)(2,1)} %collective-permute-done.10.mate_ref), custom_call_target="tpu_custom_call" | custom-call | bytes 22020096 | tf_op jit(solution)/shard_map/normalize/pallas_call | solution.py:62
  65.6 6.9 %fusion.45 = f32[1280,4]{0,1:T(4,128)S(1)} fusion(bf16[1280,4096]{1,0:T(8,128)(2,1)} %normalize.1, bf16[4,4096]{1,0:T(4,128)(2,1)S(1)} %reshape.301), kind=kOutput, calls=%fused_computation.148 | convolution fusion | flops 41943040 | bytes 10539008 | tf_op jit(solution)/shard_map/dot_general | solution.py:398
  72.5 35.7 %all-gather.2.cloned.1.call-done = bf16[4096,1536]{1,0:T(8,128)(2,1)} async-done(((bf16[64,1536]{1,0:T(8,128)(2,1)}), bf16[4096,1536]{1,0:T(8,128)(2,1)}) %all-gather.2.cloned.1.call-update) | async-done | bytes 12582928 | tf_op jit(solution)/shard_map/all_gather | solution.py:386
  108.2 2.3 %collective-permute-start.14 = (bf16[1024,512]{1,0:T(8,128)(2,1)S(1)}, bf16[1024,512]{1,0:T(8,128)(2,1)}, u32[]{:S(2)}, u32[]{:S(2)}) collective-permute-start(bf16[1024,512]{1,0:T(8,128)(2,1)S(1)} %copy-done.2), channel_id=1, source_target_pairs={{0,6},{1,25},{2,0},{3,27},{4,2},{5,29},{6,4},{7,31},{8,14},{9,1},{... | collective-permute-start | bytes 3145736 | tf_op jit(solution)/shard_map/ppermute | solution.py:41
  110.9 0.7 collective-permute-start.16
  111.7 1.2 reduce-window.21
  113.9 23.2 %convolution_convert_fusion.key_ref.left_ref.right_ref = bf16[1280,1536]{1,0:T(8,128)(2,1)} fusion(bf16[1280,4096]{1,0:T(8,128)(2,1)} %normalize.1, bf16[4096,1536]{1,0:T(8,128)(2,1)} %all-gather.2.cloned.1.call-done), kind=kOutput, calls=%fused_computation | convolution fusion | flops 16108093440 | bytes 27000832 | tf_op jit(solution)/shard_map/dot_general | solution.py:425
  137.4 2.1 %copy-done = bf16[1280,1536]{1,0:T(8,128)(2,1)S(1)} copy-done((bf16[1280,1536]{1,0:T(8,128)(2,1)S(1)}, bf16[1280,1536]{1,0:T(8,128)(2,1)}, u32[]{:S(2)}) %copy-start) | copy-done | bytes 3932184
  139.5 2.3 %states.1 = bf16[2,2,256,512]{3,2,1,0:T(8,128)(2,1)S(1)} custom-call(f32[2,640,8]{2,1,0:T(8,128)S(1)} %copy.85.cols_ref, bf16[1280,1536]{1,0:T(8,128)(2,1)S(1)} %copy-done, bf16[1280,1536]{1,0:T(8,128)(2,1)S(1)} %copy-done, bf16[1280,1536]{1,0:T(8,128)(2,1)S(1)} %copy-done), custom_call_target="tpu_custom_call" | custom-call | bytes 1024 | tf_op jit(solution)/shard_map/states/pallas_call | solution.py:225
  142.5 2.2 %collective-permute-start.18 = (bf16[2,72,512]{2,1,0:T(8,128)(2,1)S(1)}, bf16[2,72,512]{2,1,0:T(8,128)(2,1)S(1)}, u32[]{:S(2)}, u32[]{:S(2)}) collective-permute-start(bf16[2,72,512]{2,1,0:T(8,128)(2,1)S(1)} %get-tuple-element.122), channel_id=1, source_target_pairs={{0,4},{2,6},{4,0},{6,2},{1,5},{3,7},{5,1},{7,3},{8,12},{10,14},{12... | collective-permute-start | bytes 442376 | tf_op jit(solution)/shard_map/ppermute | solution.py:30
  144.7 1.1 collective-permute-start.19
  145.8 4.9 %restore.1 = bf16[4,4,4,64,512]{4,3,2,1,0:T(8,128)(2,1)} custom-call(s32[5]{0:T(128)} %concatenate.62.places, bf16[4,4,64,512]{3,2,1,0:T(8,128)(2,1)} %bitcast.165, bf16[4,4,64,512]{3,2,1,0:T(8,128)(2,1)} %bitcast.37.refs_1_, bf16[4,4,64,512]{3,2,1,0:T(8,128)(2,1)} %bitcast.38.refs_2_, bf16[4,4,64,512]{3,2,1,0:T(8,128)(2,1)} %bitcast.39.refs_3_), custom_call_target="tpu_custom_call" | custom-call | bytes 1024 | tf_op jit(solution)/shard_map/restore/pallas_call | solution.py:193
  150.7 9.5 %convolution_convert_fusion.1.query_ref = bf16[1280,512]{1,0:T(8,128)(2,1)S(1)} fusion(bf16[1280,4096]{1,0:T(8,128)(2,1)} %normalize.1, bf16[4096,512]{1,0:T(8,128)(2,1)} %bitcast.161), kind=kOutput, calls=%fused_computation.1 | convolution fusion | flops 5369364480 | bytes 15990784 | tf_op jit(solution)/shard_map/dot_general | solution.py:429
  160.3 1.0 pad_maximum_fusion
  161.7 0.8 fusion.9
  162.6 1.6 collective-permute-start.20
  164.2 2.0 collective-permute-start.21
  166.1 1.6 collective-permute-start.22
  167.8 2.1 %copy-done.1 = bf16[1280,1536]{1,0:T(8,128)(2,1)S(1)} copy-done((bf16[1280,1536]{1,0:T(8,128)(2,1)S(1)}, bf16[1280,1536]{1,0:T(8,128)(2,1)}, u32[]{:S(2)}) %copy-start.1) | copy-done | bytes 3932184
  169.9 3.7 %intra.1.intra_ref = f32[1280,1024]{1,0:T(8,128)S(1)} custom-call(f32[2,640,8]{2,1,0:T(8,128)S(1)} %copy.85.cols_ref, f32[2,8,640]{2,1,0:T(8,128)S(1)} %bitcast.157, bf16[1280,512]{1,0:T(8,128)(2,1)S(1)} %convolution_convert_fusion.1.query_ref, bf16[1280,1536]{1,0:T(8,128)(2,1)S(1)} %copy-done.1, bf16[1280,1536]{1,0:T(8,128)(2,1)S(1)} %copy-done.1, ...), custom_call_target="tpu_custom_call" | custom-call | bytes 1024 | tf_op jit(solution)/shard_map/intra/pallas_call | solution.py:265
  173.6 1.1 pad_maximum_fusion.1
  176.1 0.9 collective-permute-start.24
  177.1 1.6 collective-permute-start.25
  178.7 3.7 %collective-permute-done.23 = bf16[2,64,512]{2,1,0:T(8,128)(2,1)S(1)} collective-permute-done((bf16[2,64,512]{2,1,0:T(8,128)(2,1)S(1)}, bf16[2,64,512]{2,1,0:T(8,128)(2,1)S(1)}, u32[]{:S(2)}, u32[]{:S(2)}) %collective-permute-start.23) | collective-permute-done | bytes 131104 | tf_op jit(solution)/shard_map/ppermute | solution.py:30
  183.6 1.3 readout.3
  184.9 4.6 %collective-permute-start.26 = (bf16[640,1024]{1,0:T(8,128)(2,1)S(1)}, bf16[640,1024]{1,0:T(8,128)(2,1)S(1)}, u32[]{:S(2)}, u32[]{:S(2)}) collective-permute-start(bf16[640,1024]{1,0:T(8,128)(2,1)S(1)} %readout.3), channel_id=1, source_target_pairs={{0,1},{1,0},{2,3},{3,2},{4,5},{5,4},{6,7},{7,6},{8,9},{9,8},{10,11... | collective-permute-start | bytes 3932168 | tf_op jit(solution)/shard_map/ppermute | solution.py:26
  189.5 1.3 readout.2
  190.8 1.3 collective-permute-done.26
  192.1 2.0 %maximum_select_fusion = bf16[1,640,2048]{2,1,0:T(8,128)(2,1)} fusion(bf16[1,640,1024]{2,1,0:T(8,128)(2,1)S(1)} %bitcast.163, bf16[1,640,1024]{2,1,0:T(8,128)(2,1)S(1)} %bitcast.156, pred[]{:T(512)S(6)} %eq.88), kind=kLoop, calls=%fused_computation.2 | loop fusion | flops 11796480 | bytes 5242881 | tf_op jit(solution)/shard_map/jit(_where)/select_n | solution.py:444
  (127 shorter events, 15.1 us)
Async XLA Ops:
  6.5 101.7 %all-gather.2.cloned.1.call-start = ((), (), s32[]{:S(2)}) async-start(), calls=%async_computation | async-start | bytes 12779520 | tf_op jit(solution)/shard_map/all_gather | solution.py:386
  7.2 1.5 collective-permute-start.3
  7.9 2.0 collective-permute-start.2
  7.9 1.7 collective-permute-start
  8.4 1.5 collective-permute-start.1
  9.6 0.6 copy-start.11
  9.9 0.6 copy-start.12
  9.9 0.7 copy-start.7
  12.4 39.7 %collective-permute-start.10 = (bf16[640,4096]{1,0:T(8,128)(2,1)}, bf16[640,4096]{1,0:T(8,128)(2,1)}, u32[]{:S(2)}, u32[]{:S(2)}) collective-permute-start(bf16[640,4096]{1,0:T(8,128)(2,1)} %bitcast.158), channel_id=1, source_target_pairs={{0,1},{1,0},{2,3},{3,2},{4,5},{5,4},{6,7},{7,6},{8,9},{9,8},{10,11... | collective-permute-start | bytes 15728648 | tf_op jit(solution)/shard_map/ppermute | solution.py:26
  15.5 6.1 %collective-permute-start.4 = (bf16[80,512]{1,0:T(8,128)(2,1)}, bf16[80,512]{1,0:T(8,128)(2,1)S(1)}, u32[]{:S(2)}, u32[]{:S(2)}) collective-permute-start(bf16[80,512]{1,0:T(8,128)(2,1)} %get-tuple-element.40.refs_0_), channel_id=1, source_target_pairs={{0,96},{1,97},{2,98},{3,99},{4,100},{5,101},{6,102},{7,103},{8,104... | collective-permute-start | bytes 245768 | tf_op jit(solution)/shard_map/ppermute | solution.py:41
  16.0 5.5 %collective-permute-start.5 = (bf16[80,512]{1,0:T(8,128)(2,1)}, bf16[80,512]{1,0:T(8,128)(2,1)S(1)}, u32[]{:S(2)}, u32[]{:S(2)}) collective-permute-start(bf16[80,512]{1,0:T(8,128)(2,1)} %get-tuple-element.40.refs_0_), channel_id=1, source_target_pairs={{0,64},{1,65},{2,66},{3,67},{4,68},{5,69},{6,70},{7,71},{8,72},{9,... | collective-permute-start | bytes 245768 | tf_op jit(solution)/shard_map/ppermute | solution.py:41
  16.6 6.1 %collective-permute-start.6 = (bf16[80,512]{1,0:T(8,128)(2,1)}, bf16[80,512]{1,0:T(8,128)(2,1)S(1)}, u32[]{:S(2)}, u32[]{:S(2)}) collective-permute-start(bf16[80,512]{1,0:T(8,128)(2,1)} %get-tuple-element.40.refs_0_), channel_id=1, source_target_pairs={{0,32},{1,33},{2,34},{3,35},{4,36},{5,37},{6,38},{7,39},{8,40},{9,... | collective-permute-start | bytes 245768 | tf_op jit(solution)/shard_map/ppermute | solution.py:41
  21.6 1.1 copy-start.8
  21.6 1.1 copy-start.9
  22.7 0.6 copy-start.10
  25.8 10.4 %collective-permute-start.7 = (bf16[272,512]{1,0:T(8,128)(2,1)}, bf16[272,512]{1,0:T(8,128)(2,1)S(1)}, u32[]{:S(2)}, u32[]{:S(2)}) collective-permute-start(bf16[272,512]{1,0:T(8,128)(2,1)} %assemble.2.refs_0_), channel_id=1, source_target_pairs={{0,24},{1,7},{2,26},{3,1},{4,28},{5,3},{6,30},{7,5},{8,0},{9,15},{... | collective-permute-start | bytes 835592 | tf_op jit(solution)/shard_map/ppermute | solution.py:41
  28.4 8.3 %collective-permute-start.8 = (bf16[272,512]{1,0:T(8,128)(2,1)}, bf16[272,512]{1,0:T(8,128)(2,1)S(1)}, u32[]{:S(2)}, u32[]{:S(2)}) collective-permute-start(bf16[272,512]{1,0:T(8,128)(2,1)} %assemble.2.refs_0_), channel_id=1, source_target_pairs={{0,16},{1,5},{2,18},{3,7},{4,20},{5,1},{6,22},{7,3},{8,24},{9,13},... | collective-permute-start | bytes 835592 | tf_op jit(solution)/shard_map/ppermute | solution.py:41
  28.9 11.2 %collective-permute-start.9 = (bf16[272,512]{1,0:T(8,128)(2,1)}, bf16[272,512]{1,0:T(8,128)(2,1)S(1)}, u32[]{:S(2)}, u32[]{:S(2)}) collective-permute-start(bf16[272,512]{1,0:T(8,128)(2,1)} %assemble.2.refs_0_), channel_id=1, source_target_pairs={{0,8},{1,3},{2,10},{3,5},{4,12},{5,7},{6,14},{7,1},{8,16},{9,11},{... | collective-permute-start | bytes 835592 | tf_op jit(solution)/shard_map/ppermute | solution.py:41
  36.2 3.9 %copy-start.4 = (bf16[272,512]{1,0:T(8,128)(2,1)}, bf16[272,512]{1,0:T(8,128)(2,1)S(1)}, u32[]{:S(2)}) copy-start(bf16[272,512]{1,0:T(8,128)(2,1)S(1)} %collective-permute-done.7.refs_1_) | copy-start | bytes 835588
  36.6 3.4 %copy-start.5 = (bf16[272,512]{1,0:T(8,128)(2,1)}, bf16[272,512]{1,0:T(8,128)(2,1)S(1)}, u32[]{:S(2)}) copy-start(bf16[272,512]{1,0:T(8,128)(2,1)S(1)} %collective-permute-done.8.refs_2_) | copy-start | bytes 835588
  40.1 0.7 copy-start.6
  43.8 5.3 %collective-permute-start.11 = (bf16[16,512]{1,0:T(8,128)(2,1)}, bf16[16,512]{1,0:T(8,128)(2,1)S(1)}, u32[]{:S(2)}, u32[]{:S(2)}) collective-permute-start(bf16[16,512]{1,0:T(8,128)(2,1)} %get-tuple-element.52), channel_id=1, source_target_pairs={{0,6},{1,25},{2,0},{3,27},{4,2},{5,29},{6,4},{7,31},{8,14},{9,1},{... | collective-permute-start | bytes 49160 | tf_op jit(solution)/shard_map/ppermute | solution.py:41
  46.6 4.3 %collective-permute-start.12 = (bf16[16,512]{1,0:T(8,128)(2,1)}, bf16[16,512]{1,0:T(8,128)(2,1)S(1)}, u32[]{:S(2)}, u32[]{:S(2)}) collective-permute-start(bf16[16,512]{1,0:T(8,128)(2,1)} %get-tuple-element.52), channel_id=1, source_target_pairs={{0,4},{1,17},{2,6},{3,19},{4,0},{5,21},{6,2},{7,23},{8,12},{9,25},... | collective-permute-start | bytes 49160 | tf_op jit(solution)/shard_map/ppermute | solution.py:41
  46.6 4.4 %collective-permute-start.13 = (bf16[16,512]{1,0:T(8,128)(2,1)}, bf16[16,512]{1,0:T(8,128)(2,1)S(1)}, u32[]{:S(2)}, u32[]{:S(2)}) collective-permute-start(bf16[16,512]{1,0:T(8,128)(2,1)} %get-tuple-element.52), channel_id=1, source_target_pairs={{0,2},{1,9},{2,4},{3,11},{4,6},{5,13},{6,0},{7,15},{8,10},{9,17},{... | collective-permute-start | bytes 49160 | tf_op jit(solution)/shard_map/ppermute | solution.py:41
  65.6 42.6 %copy-start.2 = (bf16[1024,512]{1,0:T(8,128)(2,1)S(1)}, bf16[1024,512]{1,0:T(8,128)(2,1)}, u32[]{:S(2)}) copy-start(bf16[1024,512]{1,0:T(8,128)(2,1)} %get-tuple-element.62) | copy-start | bytes 3145732
  108.2 33.6 %collective-permute-start.14 = (bf16[1024,512]{1,0:T(8,128)(2,1)S(1)}, bf16[1024,512]{1,0:T(8,128)(2,1)}, u32[]{:S(2)}, u32[]{:S(2)}) collective-permute-start(bf16[1024,512]{1,0:T(8,128)(2,1)S(1)} %copy-done.2), channel_id=1, source_target_pairs={{0,6},{1,25},{2,0},{3,27},{4,2},{5,29},{6,4},{7,31},{8,14},{9,1},{... | collective-permute-start | bytes 3145736 | tf_op jit(solution)/shard_map/ppermute | solution.py:41
  110.5 31.3 %collective-permute-start.15 = (bf16[1024,512]{1,0:T(8,128)(2,1)S(1)}, bf16[1024,512]{1,0:T(8,128)(2,1)}, u32[]{:S(2)}, u32[]{:S(2)}) collective-permute-start(bf16[1024,512]{1,0:T(8,128)(2,1)S(1)} %copy-done.2), channel_id=1, source_target_pairs={{0,4},{1,17},{2,6},{3,19},{4,0},{5,21},{6,2},{7,23},{8,12},{9,25},... | collective-permute-start | bytes 3145736 | tf_op jit(solution)/shard_map/ppermute | solution.py:41
  110.9 30.9 %collective-permute-start.16 = (bf16[1024,512]{1,0:T(8,128)(2,1)S(1)}, bf16[1024,512]{1,0:T(8,128)(2,1)}, u32[]{:S(2)}, u32[]{:S(2)}) collective-permute-start(bf16[1024,512]{1,0:T(8,128)(2,1)S(1)} %copy-done.2), channel_id=1, source_target_pairs={{0,2},{1,9},{2,4},{3,11},{4,6},{5,13},{6,0},{7,15},{8,10},{9,17},{... | collective-permute-start | bytes 3145736 | tf_op jit(solution)/shard_map/ppermute | solution.py:41
  137.4 2.1 %copy-start = (bf16[1280,1536]{1,0:T(8,128)(2,1)S(1)}, bf16[1280,1536]{1,0:T(8,128)(2,1)}, u32[]{:S(2)}) copy-start(bf16[1280,1536]{1,0:T(8,128)(2,1)} %convolution_convert_fusion.key_ref.left_ref.right_ref) | copy-start | bytes 11796484
  142.4 17.9 %collective-permute-start.17 = (bf16[2,72,512]{2,1,0:T(8,128)(2,1)S(1)}, bf16[2,72,512]{2,1,0:T(8,128)(2,1)S(1)}, u32[]{:S(2)}, u32[]{:S(2)}) collective-permute-start(bf16[2,72,512]{2,1,0:T(8,128)(2,1)S(1)} %get-tuple-element.121), channel_id=1, source_target_pairs={{0,2},{2,4},{4,6},{6,0},{1,3},{3,5},{5,7},{7,1},{8,10},{10,12},{12... | collective-permute-start | bytes 442376 | tf_op jit(solution)/shard_map/ppermute | solution.py:30
  142.5 17.8 %collective-permute-start.18 = (bf16[2,72,512]{2,1,0:T(8,128)(2,1)S(1)}, bf16[2,72,512]{2,1,0:T(8,128)(2,1)S(1)}, u32[]{:S(2)}, u32[]{:S(2)}) collective-permute-start(bf16[2,72,512]{2,1,0:T(8,128)(2,1)S(1)} %get-tuple-element.122), channel_id=1, source_target_pairs={{0,4},{2,6},{4,0},{6,2},{1,5},{3,7},{5,1},{7,3},{8,12},{10,14},{12... | collective-permute-start | bytes 442376 | tf_op jit(solution)/shard_map/ppermute | solution.py:30
  144.7 15.6 %collective-permute-start.19 = (bf16[2,72,512]{2,1,0:T(8,128)(2,1)S(1)}, bf16[2,72,512]{2,1,0:T(8,128)(2,1)}, u32[]{:S(2)}, u32[]{:S(2)}) collective-permute-start(bf16[2,72,512]{2,1,0:T(8,128)(2,1)S(1)} %get-tuple-element.123), channel_id=1, source_target_pairs={{0,6},{2,0},{4,2},{6,4},{1,7},{3,1},{5,3},{7,5},{8,14},{10,8},{12,... | collective-permute-start | bytes 442376 | tf_op jit(solution)/shard_map/ppermute | solution.py:30
  162.6 11.0 %collective-permute-start.20 = (bf16[2,72,512]{2,1,0:T(8,128)(2,1)S(1)}, bf16[2,72,512]{2,1,0:T(8,128)(2,1)}, u32[]{:S(2)}, u32[]{:S(2)}) collective-permute-start(bf16[2,72,512]{2,1,0:T(8,128)(2,1)S(1)} %pad_maximum_fusion.9), channel_id=1, source_target_pairs={{0,8},{8,16},{16,24},{24,0},{1,9},{9,17},{17,25},{25,1},{2,10},{10... | collective-permute-start | bytes 442376 | tf_op jit(solution)/shard_map/ppermute | solution.py:30
  164.2 9.4 %collective-permute-start.21 = (bf16[2,72,512]{2,1,0:T(8,128)(2,1)S(1)}, bf16[2,72,512]{2,1,0:T(8,128)(2,1)}, u32[]{:S(2)}, u32[]{:S(2)}) collective-permute-start(bf16[2,72,512]{2,1,0:T(8,128)(2,1)S(1)} %pad_maximum_fusion.9), channel_id=1, source_target_pairs={{0,16},{8,24},{16,0},{24,8},{1,17},{9,25},{17,1},{25,9},{2,18},{10... | collective-permute-start | bytes 442376 | tf_op jit(solution)/shard_map/ppermute | solution.py:30
  166.1 7.5 %collective-permute-start.22 = (bf16[2,72,512]{2,1,0:T(8,128)(2,1)S(1)}, bf16[2,72,512]{2,1,0:T(8,128)(2,1)}, u32[]{:S(2)}, u32[]{:S(2)}) collective-permute-start(bf16[2,72,512]{2,1,0:T(8,128)(2,1)S(1)} %pad_maximum_fusion.9), channel_id=1, source_target_pairs={{0,24},{8,0},{16,8},{24,16},{1,25},{9,1},{17,9},{25,17},{2,26},{10... | collective-permute-start | bytes 442376 | tf_op jit(solution)/shard_map/ppermute | solution.py:30
  167.7 2.1 %copy-start.1 = (bf16[1280,1536]{1,0:T(8,128)(2,1)S(1)}, bf16[1280,1536]{1,0:T(8,128)(2,1)}, u32[]{:S(2)}) copy-start(bf16[1280,1536]{1,0:T(8,128)(2,1)} %convolution_convert_fusion.key_ref.left_ref.right_ref) | copy-start | bytes 11796484
  169.9 5.6 %copy-start.3 = (bf16[2,64,512]{2,1,0:T(8,128)(2,1)S(1)}, bf16[2,64,512]{2,1,0:T(8,128)(2,1)}, u32[]{:S(2)}) copy-start(bf16[2,64,512]{2,1,0:T(8,128)(2,1)} %get-tuple-element.79) | copy-start | bytes 393220
  175.8 6.5 %collective-permute-start.23 = (bf16[2,64,512]{2,1,0:T(8,128)(2,1)S(1)}, bf16[2,64,512]{2,1,0:T(8,128)(2,1)S(1)}, u32[]{:S(2)}, u32[]{:S(2)}) collective-permute-start(bf16[2,64,512]{2,1,0:T(8,128)(2,1)S(1)} %get-tuple-element.105), channel_id=1, source_target_pairs={{0,2},{2,4},{4,6},{6,0},{1,3},{3,5},{5,7},{7,1},{8,10},{10,12},{12... | collective-permute-start | bytes 393224 | tf_op jit(solution)/shard_map/ppermute | solution.py:30
  176.1 6.2 %collective-permute-start.24 = (bf16[2,64,512]{2,1,0:T(8,128)(2,1)S(1)}, bf16[2,64,512]{2,1,0:T(8,128)(2,1)S(1)}, u32[]{:S(2)}, u32[]{:S(2)}) collective-permute-start(bf16[2,64,512]{2,1,0:T(8,128)(2,1)S(1)} %get-tuple-element.104), channel_id=1, source_target_pairs={{0,4},{2,6},{4,0},{6,2},{1,5},{3,7},{5,1},{7,3},{8,12},{10,14},{12... | collective-permute-start | bytes 393224 | tf_op jit(solution)/shard_map/ppermute | solution.py:30
  177.1 5.9 %collective-permute-start.25 = (bf16[2,64,512]{2,1,0:T(8,128)(2,1)S(1)}, bf16[2,64,512]{2,1,0:T(8,128)(2,1)S(1)}, u32[]{:S(2)}, u32[]{:S(2)}) collective-permute-start(bf16[2,64,512]{2,1,0:T(8,128)(2,1)S(1)} %get-tuple-element.103), channel_id=1, source_target_pairs={{0,6},{2,0},{4,2},{6,4},{1,7},{3,1},{5,3},{7,5},{8,14},{10,8},{12,... | collective-permute-start | bytes 393224 | tf_op jit(solution)/shard_map/ppermute | solution.py:30
  184.9 7.2 %collective-permute-start.26 = (bf16[640,1024]{1,0:T(8,128)(2,1)S(1)}, bf16[640,1024]{1,0:T(8,128)(2,1)S(1)}, u32[]{:S(2)}, u32[]{:S(2)}) collective-permute-start(bf16[640,1024]{1,0:T(8,128)(2,1)S(1)} %readout.3), channel_id=1, source_target_pairs={{0,1},{1,0},{2,3},{3,2},{4,5},{5,4},{6,7},{7,6},{8,9},{9,8},{10,11... | collective-permute-start | bytes 3932168 | tf_op jit(solution)/shard_map/ppermute | solution.py:26
Sparse Core Ops, SparseCore 0:
  12.5 95.6 all-gather.1
